TPU v7x, 256 devices: a whole 4x4x8 slice. The times are simulated.
256 devices in a mesh: ctx: 64 (over y, x, z_hi, core), grp: 4 (over z_lo).
Axes of the slice: x: 4, y: 4, z: 8 (z_hi: 2, z_lo: 4; z = z_hi * 4 + z_lo), core: 2. Of those that a mesh axis runs over, the one named last changes fastest.
Arguments:
- query_in: float32 [1024, 16384], P('grp', 'ctx'), may hold values from -6 to 6
- key_in: float32 [1024, 16384], P('grp', 'ctx'), may hold values from -6 to 6
- value_in: float32 [1024, 16384], P('grp', 'ctx'), may hold values from -6 to 6
- short_weight: float32 [3, 7, 1024], P(None, None, 'grp'), may hold values from -2 to 2
- long_filter: float32 [1024, 16384], P('grp', 'ctx'), may hold values from -1.1 to 1.1
- skip_weight: float32 [1024], P('grp'), may hold values from -4 to 4
Outputs:
- mixed: float32 [1024, 16384], P('grp', 'ctx')
All inputs are finite; a program needn't handle non-finite values.
Results may differ from a plain program's by a relative error of at most 0.00012.
Values sent between devices are 32-bit elements; how exact they have to be, the bound alone decides.
No kernel may reach another device: no remote copies, remote signals or barrier semaphores. Data moves between devices by JAX's collectives and lax.ppermute only.
A program may use at most 64 MiB of HBM per device.

v0:
```python
import math

import jax
import jax.numpy as jnp
from jax import lax
from jax.sharding import PartitionSpec as P


def shifted(block, axis, distance):
    devices = range(lax.axis_size(axis))
    route = [(i - distance, i) for i in devices if i - distance in devices]
    return lax.ppermute(block, axis, route)


def causal_taps(stream, prior, weights):
    seq_len = stream.shape[1]
    rim_width = weights.shape[0] - 1
    padded = jnp.concatenate([prior, stream], axis=1)
    total = weights[0][:, None] * padded[:, rim_width : rim_width + seq_len]
    for offset in range(1, weights.shape[0]):
        total = (
            total
            + weights[offset][:, None]
            * padded[:, rim_width - offset : rim_width - offset + seq_len]
        )
    return total


def dft_tables(order):
    indices = jnp.arange(order, dtype=jnp.int32)
    phase = indices[:, None] * indices[None, :] % order
    angle = phase.astype(jnp.float32) * (2.0 * math.pi / order)
    return (jnp.cos(angle), jnp.sin(angle))


def forward_spectrum(
    signal, row_order, col_order, row_table, twist_cos, twist_sin, cols_real, cols_imag
):
    channels = signal.shape[0]
    half_rows = row_order // 2
    highest = lax.Precision.HIGHEST
    flat = (
        signal.reshape(channels, half_rows, col_order)
        .transpose(1, 0, 2)
        .reshape(half_rows, channels * col_order)
    )
    first = jnp.dot(row_table, flat, precision=highest)
    first_real = first[:row_order].reshape(row_order, channels, col_order)
    first_imag = first[row_order:].reshape(row_order, channels, col_order)
    turn_real = (first_real * twist_cos + first_imag * twist_sin).reshape(
        row_order * channels, col_order
    )
    turn_imag = (first_imag * twist_cos - first_real * twist_sin).reshape(
        row_order * channels, col_order
    )
    return jnp.dot(turn_real, cols_real, precision=highest) + jnp.dot(
        turn_imag, cols_imag, precision=highest
    )


def long_conv(signal, taps_block):
    channels = signal.shape[0]
    seq_len = signal.shape[1]
    padded_len = 2 * seq_len
    row_order = 1
    while row_order * row_order < padded_len and padded_len % (2 * row_order) == 0:
        row_order = row_order * 2
    col_order = padded_len // row_order
    half_rows = row_order // 2
    highest = lax.Precision.HIGHEST
    cos_rows, sin_rows = dft_tables(row_order)
    cos_cols, sin_cols = dft_tables(col_order)
    row_index = jnp.arange(row_order, dtype=jnp.int32)
    col_index = jnp.arange(col_order, dtype=jnp.int32)
    twist_angle = (row_index[:, None] * col_index[None, :] % padded_len).astype(jnp.float32) * (
        2.0 * math.pi / padded_len
    )
    twist_cos = jnp.cos(twist_angle)[:, None, :]
    twist_sin = jnp.sin(twist_angle)[:, None, :]
    row_table = jnp.concatenate([cos_rows[:, :half_rows], -sin_rows[:, :half_rows]], axis=0)
    fwd_real = jnp.concatenate([cos_cols, -sin_cols], axis=1)
    fwd_imag = jnp.concatenate([sin_cols, cos_cols], axis=1)
    sig_spec = forward_spectrum(
        signal, row_order, col_order, row_table, twist_cos, twist_sin, fwd_real, fwd_imag
    )
    filt_spec = forward_spectrum(
        taps_block, row_order, col_order, row_table, twist_cos, twist_sin, fwd_real, fwd_imag
    )
    sig_real, sig_imag = (sig_spec[:, :col_order], sig_spec[:, col_order:])
    filt_real, filt_imag = (filt_spec[:, :col_order], filt_spec[:, col_order:])
    prod_real = sig_real * filt_real - sig_imag * filt_imag
    prod_imag = sig_real * filt_imag + sig_imag * filt_real
    inv_real = jnp.concatenate([cos_cols, sin_cols], axis=1)
    inv_imag = jnp.concatenate([-sin_cols, cos_cols], axis=1)
    back = jnp.dot(prod_real, inv_real, precision=highest) + jnp.dot(
        prod_imag, inv_imag, precision=highest
    )
    back_real = back[:, :col_order].reshape(row_order, channels, col_order)
    back_imag = back[:, col_order:].reshape(row_order, channels, col_order)
    undo_real = (back_real * twist_cos - back_imag * twist_sin).reshape(
        row_order, channels * col_order
    )
    undo_imag = (back_real * twist_sin + back_imag * twist_cos).reshape(
        row_order, channels * col_order
    )
    result = jnp.dot(cos_rows[:half_rows], undo_real, precision=highest) - jnp.dot(
        sin_rows[:half_rows], undo_imag, precision=highest
    )
    result = result.reshape(half_rows, channels, col_order).transpose(1, 0, 2)
    return result.reshape(channels, seq_len) / padded_len


def on_device(query_in, key_in, value_in, short_weight, long_filter, skip_weight):
    rim_width = short_weight.shape[1] - 1
    group_width = query_in.shape[0]
    seq_rows = query_in.shape[1]
    edges = jnp.stack(
        [
            query_in[:, seq_rows - rim_width :],
            key_in[:, seq_rows - rim_width :],
            value_in[:, seq_rows - rim_width :],
        ]
    )
    before = shifted(edges, "ctx", 1)
    query = causal_taps(query_in, before[0], short_weight[0])
    keyed = causal_taps(key_in, before[1], short_weight[1])
    valued = causal_taps(value_in, before[2], short_weight[2])
    gated = keyed * valued
    shards = lax.axis_size("ctx")
    per_device = group_width // shards
    gated_split = gated.reshape(shards, per_device, seq_rows)
    filter_split = long_filter.reshape(shards, per_device, seq_rows)
    moved_gated, moved_filter = (
        lax.all_to_all(gated_split, "ctx", split_axis=0, concat_axis=2, tiled=True),
        lax.all_to_all(filter_split, "ctx", split_axis=0, concat_axis=2, tiled=True),
    )
    convolved = long_conv(moved_gated[0], moved_filter[0])
    returned = lax.all_to_all(convolved[None], "ctx", split_axis=2, concat_axis=0, tiled=True)
    conv_local = returned.reshape(group_width, seq_rows)
    return query * (conv_local + skip_weight[:, None] * gated)


def solution(mesh):
    return jax.shard_map(
        on_device,
        mesh=mesh,
        in_specs=(
            P("grp", "ctx"),
            P("grp", "ctx"),
            P("grp", "ctx"),
            P(None, None, "grp"),
            P("grp", "ctx"),
            P("grp"),
        ),
        out_specs=P("grp", "ctx"),
        check_vma=False,
    )
```

profile of v0, /device:TPU:33, one launch (start us, length us, event | category | flops | bytes accessed | tf_op | source)
XLA Modules:
  0.0 206.9 jit_solution(14746826805699046638)
XLA Ops:
  0.0 1.0 slice.224
  1.0 0.1 copy.23
  1.1 1.0 slice.225
  2.1 0.1 copy.24
  2.2 1.0 slice.226
  3.2 0.1 copy.25
  3.3 8.5 %collective-permute-start = (f32[3,256,6]{1,2,0:T(8,128)S(1)}, f32[3,256,6]{1,2,0:T(8,128)S(1)}, u32[]{:S(2)}, u32[]{:S(2)}) collective-permute-start(f32[3,256,6]{1,2,0:T(8,128)S(1)} %pad_maximum_fusion.16), channel_id=1, source_target_pairs={{0,4},{4,8},{8,12},{12,16},{16,20},{20,24},{24,28},{28,32},{32,36}... | collective-permute-start | bytes 55304 | tf_op jit(solution)/shard_map/ppermute | solution.py:12
  11.8 1.7 reshape.184
  13.5 7.6 %all-to-all-start.1 = ((f32[64,4,256]{2,1,0:T(4,128)}), f32[64,4,256]{2,1,0:T(4,128)S(1)}, u32[]{:S(2)}, u32[]{:S(2)}) async-start(f32[64,4,256]{2,1,0:T(4,128)} %reshape.184), calls=%async_computation.1 | async-start | bytes 524288 | tf_op jit(solution)/shard_map/all_to_all | solution.py:135
  21.1 1.6 fusion.134
  22.7 0.8 fusion.135
  23.5 1.0 fusion.110
  24.4 1.0 fusion.109
  25.4 0.3 fusion.121
  25.7 0.5 fusion.118
  26.2 0.5 fusion.117
  26.7 0.3 fusion.120
  27.0 0.0 collective-permute-done
  27.1 0.1 copy.15
  27.2 0.1 copy.16
  27.4 4.4 %fusion.46 = f32[256,256]{1,0:T(8,128)S(1)} fusion(f32[256,256]{1,0:T(8,128)} %param.8, f32[256,256]{1,0:T(8,128)} %param.7, f32[256,6]{1,0:T(8,128)S(1)} %copy.16, f32[256,6]{1,0:T(8,128)S(1)} %copy.15, f32[256]{0:T(256)S(1)} %bitcast.120, f32[256]{0:T(256)S(1)} %bitcast.119, f32[256]{0:T(256)S(1)} %bitcast.107, f32[256]{0:T(256)S(1)} %bitcast.108, ...), kind=kLoop, calls=%fused_computation.85 | loop fusion | flops 2555904 | bytes 813056 | tf_op jit(solution)/shard_map/mul | solution.py:128
  31.7 0.8 reshape.180
  32.5 5.1 %all-to-all-done.1 = f32[64,4,256]{2,1,0:T(4,128)S(1)} async-done(((f32[64,4,256]{2,1,0:T(4,128)}), f32[64,4,256]{2,1,0:T(4,128)S(1)}, u32[]{:S(2)}, u32[]{:S(2)}) %all-to-all-start.1) | async-done | bytes 262176 | tf_op jit(solution)/shard_map/all_to_all | solution.py:135
  37.6 7.9 %all-to-all-start = ((f32[64,4,256]{2,1,0:T(4,128)}), f32[64,4,256]{2,1,0:T(4,128)}, u32[]{:S(2)}, u32[]{:S(2)}) async-start(f32[64,4,256]{2,1,0:T(4,128)} %reshape.180), calls=%async_computation | async-start | bytes 524288 | tf_op jit(solution)/shard_map/all_to_all | solution.py:134
  45.5 0.1 copy.19
  45.6 0.1 copy.20
  45.7 1.0 fusion.98
  46.7 0.1 fusion.133
  46.9 0.1 mul.681
  47.0 0.1 mul.684
  47.1 0.0 copy-done.2
  47.1 1.0 fusion.16
  48.1 1.0 convolution_add_fusion.1
  49.0 12.8 %all-to-all-done = f32[64,4,256]{2,1,0:T(4,128)} async-done(((f32[64,4,256]{2,1,0:T(4,128)}), f32[64,4,256]{2,1,0:T(4,128)}, u32[]{:S(2)}, u32[]{:S(2)}) %all-to-all-start) | async-done | bytes 262176 | tf_op jit(solution)/shard_map/all_to_all | solution.py:134
  61.8 1.0 copy.17
  62.9 0.1 copy.18
  63.0 2.0 fusion.99
  65.0 0.9 fusion.132
  65.9 1.1 reshape.183
  67.0 1.9 fusion.23
  68.9 1.0 convolution_add_fusion.2
  69.9 1.0 fusion.9
  70.9 1.0 convolution_add_fusion
  71.8 0.1 fusion.131
  71.9 0.1 reshape.188
  72.0 0.1 reshape.189
  72.1 0.0 copy-done.5
  72.1 0.5 fusion.2
  72.6 0.5 fusion
  73.1 0.1 div.14
  73.2 4.9 %copy.21 = f32[4,128,128]{0,2,1:T(8,128)} copy(f32[4,128,128]{2,0,1:T(4,128)S(1)} %bitcast.91) | data formatting | bytes 524288 | tf_op jit(solution)/shard_map/div | solution.py:110
  78.1 0.5 broadcast.113
  78.6 74.6 %reduce = f32[16384,4]{1,0:T(8,128)} reduce(f32[16384,1,4]{2,1,0:T(1,128)} %bitcast.77, f32[]{:T(128)} %broadcast.113), dimensions={1}, to_apply=%bitcast.73.reduce_sub_computation | reduce | bytes 524292
  153.2 9.1 %reshape.191 = f32[64,1,1024]{2,1,0:T(1,128)} reshape(f32[16384,4]{1,0:T(8,128)} %reduce) | data formatting | bytes 524288
  162.3 4.5 %all-to-all-start.2 = ((f32[64,1,1024]{2,1,0:T(1,128)}), f32[64,1,1024]{2,1,0:T(1,128)S(1)}, u32[]{:S(2)}, u32[]{:S(2)}) async-start(f32[64,1,1024]{2,1,0:T(1,128)} %reshape.191), calls=%async_computation.2 | async-start | bytes 524288 | tf_op jit(solution)/shard_map/all_to_all | solution.py:138
  166.8 0.1 copy.14
  167.0 16.7 %all-to-all-done.2 = f32[64,1,1024]{2,1,0:T(1,128)S(1)} async-done(((f32[64,1,1024]{2,1,0:T(1,128)}), f32[64,1,1024]{2,1,0:T(1,128)S(1)}, u32[]{:S(2)}, u32[]{:S(2)}) %all-to-all-start.2) | async-done | bytes 262176 | tf_op jit(solution)/shard_map/all_to_all | solution.py:138
  183.7 1.2 reduce.1
  184.9 0.0 copy-start.8
  184.9 0.0 copy-start.14
  184.9 14.8 %reshape.192 = f32[16384,1,4]{2,1,0:T(1,128)} reshape(f32[64,1024]{1,0:T(8,128)S(1)} %reduce.1) | data formatting | bytes 524288
  199.7 5.3 %copy.22 = f32[64,1,4,256]{3,2,0,1:T(4,128)S(1)} copy(f32[64,1,4,256]{2,3,0,1:T(8,128)} %bitcast.78) | data formatting | bytes 524288 | tf_op jit(solution)/shard_map/all_to_all | solution.py:138
  205.1 0.1 reshape.190
  205.2 1.6 fusion.79
  (35 shorter events, 0.2 us)
Async XLA Ops:
  3.3 23.8 %collective-permute-start = (f32[3,256,6]{1,2,0:T(8,128)S(1)}, f32[3,256,6]{1,2,0:T(8,128)S(1)}, u32[]{:S(2)}, u32[]{:S(2)}) collective-permute-start(f32[3,256,6]{1,2,0:T(8,128)S(1)} %pad_maximum_fusion.16), channel_id=1, source_target_pairs={{0,4},{4,8},{8,12},{12,16},{16,20},{20,24},{24,28},{28,32},{32,36}... | collective-permute-start | bytes 55304 | tf_op jit(solution)/shard_map/ppermute | solution.py:12
  13.5 24.1 %all-to-all-start.1 = ((f32[64,4,256]{2,1,0:T(4,128)}), f32[64,4,256]{2,1,0:T(4,128)S(1)}, u32[]{:S(2)}, u32[]{:S(2)}) async-start(f32[64,4,256]{2,1,0:T(4,128)} %reshape.184), calls=%async_computation.1 | async-start | bytes 524288 | tf_op jit(solution)/shard_map/all_to_all | solution.py:135
  24.4 2.9 %copy-start.4 = (f32[256,256]{1,0:T(8,128)}, f32[256,256]{1,0:T(8,128)S(1)}, u32[]{:S(2)}) copy-start(f32[256,256]{1,0:T(8,128)S(1)} %fusion.110) | copy-start | bytes 786436
  25.4 20.0 %copy-start.6 = (f32[256,256]{1,0:T(8,128)}, f32[256,256]{1,0:T(8,128)S(1)}, u32[]{:S(2)}) copy-start(f32[256,256]{1,0:T(8,128)S(1)} %fusion.109) | copy-start | bytes 786436
  25.7 21.4 %copy-start.2 = (f32[128,128]{1,0:T(8,128)}, f32[128,128]{1,0:T(8,128)S(1)}, u32[]{:S(2)}) copy-start(f32[128,128]{1,0:T(8,128)S(1)} %get-tuple-element.36) | copy-start | bytes 196612
  26.7 19.0 %copy-start = (f32[256,128]{1,0:T(8,128)}, f32[256,128]{1,0:T(8,128)S(1)}, u32[]{:S(2)}) copy-start(f32[256,128]{1,0:T(8,128)S(1)} %slice_negate_fusion) | copy-start | bytes 393220
  27.0 18.7 %copy-start.1 = (f32[256,128]{1,0:T(8,128)}, f32[256,128]{1,0:T(8,128)S(1)}, u32[]{:S(2)}) copy-start(f32[256,128]{1,0:T(8,128)S(1)} %slice.293) | copy-start | bytes 393220
  37.6 24.3 %all-to-all-start = ((f32[64,4,256]{2,1,0:T(4,128)}), f32[64,4,256]{2,1,0:T(4,128)}, u32[]{:S(2)}, u32[]{:S(2)}) async-start(f32[64,4,256]{2,1,0:T(4,128)} %reshape.180), calls=%async_computation | async-start | bytes 524288 | tf_op jit(solution)/shard_map/all_to_all | solution.py:134
  67.0 3.9 %copy-start.3 = (f32[128,128]{1,0:T(8,128)S(1)}, f32[128,128]{1,0:T(8,128)}, u32[]{:S(2)}) copy-start(f32[128,128]{1,0:T(8,128)} %copy-done.2) | copy-start | bytes 196612
  69.8 2.3 %copy-start.5 = (f32[256,256]{1,0:T(8,128)S(1)}, f32[256,256]{1,0:T(8,128)}, u32[]{:S(2)}) copy-start(f32[256,256]{1,0:T(8,128)} %copy-done.4) | copy-start | bytes 786436
  69.9 2.7 %copy-start.7 = (f32[256,256]{1,0:T(8,128)S(1)}, f32[256,256]{1,0:T(8,128)}, u32[]{:S(2)}) copy-start(f32[256,256]{1,0:T(8,128)} %copy-done.6) | copy-start | bytes 786436
  162.3 21.4 %all-to-all-start.2 = ((f32[64,1,1024]{2,1,0:T(1,128)}), f32[64,1,1024]{2,1,0:T(1,128)S(1)}, u32[]{:S(2)}, u32[]{:S(2)}) async-start(f32[64,1,1024]{2,1,0:T(1,128)} %reshape.191), calls=%async_computation.2 | async-start | bytes 524288 | tf_op jit(solution)/shard_map/all_to_all | solution.py:138
  184.9 20.3 %copy-start.8 = (f32[256,256]{1,0:T(8,128)S(1)}, f32[256,256]{1,0:T(8,128)}, u32[]{:S(2)}) copy-start(f32[256,256]{1,0:T(8,128)} %param.6) | copy-start | bytes 786436
  184.9 20.3 %copy-start.9 = (f32[1,1,256]{2,1,0:T(1,128)S(1)}, f32[1,1,256]{2,1,0:T(1,128)}, u32[]{:S(2)}) copy-start(f32[1,1,256]{2,1,0:T(1,128)} %get-tuple-element.25) | copy-start | bytes 3076
  184.9 20.3 %copy-start.10 = (f32[1,1,256]{2,1,0:T(1,128)S(1)}, f32[1,1,256]{2,1,0:T(1,128)}, u32[]{:S(2)}) copy-start(f32[1,1,256]{2,1,0:T(1,128)} %get-tuple-element.26) | copy-start | bytes 3076
  184.9 20.3 %copy-start.11 = (f32[1,1,256]{2,1,0:T(1,128)S(1)}, f32[1,1,256]{2,1,0:T(1,128)}, u32[]{:S(2)}) copy-start(f32[1,1,256]{2,1,0:T(1,128)} %get-tuple-element.27) | copy-start | bytes 3076
  184.9 20.3 %copy-start.12 = (f32[1,1,256]{2,1,0:T(1,128)S(1)}, f32[1,1,256]{2,1,0:T(1,128)}, u32[]{:S(2)}) copy-start(f32[1,1,256]{2,1,0:T(1,128)} %get-tuple-element.28) | copy-start | bytes 3076
  184.9 20.3 %copy-start.13 = (f32[1,1,256]{2,1,0:T(1,128)S(1)}, f32[1,1,256]{2,1,0:T(1,128)}, u32[]{:S(2)}) copy-start(f32[1,1,256]{2,1,0:T(1,128)} %get-tuple-element.29) | copy-start | bytes 3076
  184.9 20.3 %copy-start.14 = (f32[256]{0:T(256)S(1)}, f32[256]{0:T(256)}, u32[]{:S(2)}) copy-start(f32[256]{0:T(256)} %param.11) | copy-start | bytes 3076
where the time goes:
time: 208 us; the launch traced here: 207 us
  other arithmetic  85.3 us (41%)
  local copies, waits for them, and re-layouts  47.3 us (23%)
  waiting for transfers between devices  34.6 us (17%)
  starting transfers between devices  28.5 us (14%)
  matrix products  10.7 us (5%)
    unnamed x1, other arithmetic  74.6 us
    unnamed x36, local copies, waits for them, and re-layouts  24.7 us
    all_to_all x1, waiting for transfers between devices, on_device(): lax.all_to_all(convolved[None], 'ctx', split_axis=2, concat_axis=0, tiled...  16.7 us
    all_to_all x1, waiting for transfers between devices, on_device(): lax.all_to_all(gated_split, 'ctx', split_axis=0, concat_axis=2, tiled=True)  12.8 us
    ppermute x1, starting transfers between devices, shifted(): return lax.ppermute(block, axis, route)  8.48 us
    all_to_all x1, starting transfers between devices, on_device(): lax.all_to_all(gated_split, 'ctx', split_axis=0, concat_axis=2, tiled=True)  7.85 us
    all_to_all x1, starting transfers between devices, on_device(): lax.all_to_all(filter_split, 'ctx', split_axis=0, concat_axis=2, tiled=True)  7.6 us
    all_to_all x1, local copies, waits for them, and re-layouts, on_device(): lax.all_to_all(convolved[None], 'ctx', split_axis=2, concat_axis=0, tiled...  5.34 us
  transfers between devices with their start and end apart: 4, of which 3 were waited for; matrix products, arithmetic and copies ran while one was open for 8% of the time, Pallas kernels for 0%

commit v1 on v0

v1 whole, which is shorter than its diff:
```python
import math

import jax
import jax.numpy as jnp
import ml_dtypes
import numpy as np
from jax import lax
from jax.experimental import pallas as pl
from jax.experimental.pallas import tpu as pltpu
from jax.sharding import PartitionSpec as P

LANES = 128
F32 = jnp.float32
BF16 = jnp.bfloat16
VMEM = pl.BlockSpec(memory_space=pltpu.VMEM)
SMEM = pl.BlockSpec(memory_space=pltpu.SMEM)


def halves(table):
    high = table.astype(ml_dtypes.bfloat16)
    low = (table - high.astype(np.float64)).astype(ml_dtypes.bfloat16)
    return high, low


def split(x):
    high = x.astype(BF16)
    return high, (x - high.astype(F32)).astype(BF16)


def tables(blocks, width):
    odd = 2 * np.arange(blocks) + 1
    angle = 2.0 * math.pi * (odd[:, None] * np.arange(blocks)[None, :] % (4 * blocks)) / (4 * blocks)
    high, low = halves(np.concatenate([np.cos(angle), np.sin(angle)], axis=0))
    rows_in = np.concatenate([high, high, low], axis=1)
    scale = 1.0 / (blocks * width)
    high, low = halves(np.concatenate([np.cos(angle), np.sin(angle)], axis=0).T * scale)
    rows_out = np.concatenate([high, high, low], axis=1)
    order = 4 * blocks * width
    turn = 2.0 * math.pi * (odd[:, None] * np.arange(width)[None, :] % order) / order
    index = np.arange(width)
    phase = 2.0 * math.pi * (index[:, None] * index[None, :] % width) / width
    high, low = halves(np.stack([np.cos(phase), np.sin(phase), -np.sin(phase)]))
    return (
        rows_in,
        rows_out,
        np.stack([np.cos(turn), np.sin(turn)]).astype(np.float32),
        high,
        low,
    )


def tap_columns(weights):
    taps, channels = weights.shape
    padded = jnp.concatenate([weights, jnp.zeros((LANES - taps, channels), F32)], axis=0)
    return padded.T


def taps_of_rows(left, right, columns, taps):
    lane = lax.broadcasted_iota(jnp.int32, left.shape, 1)
    weight = columns[:, 0:1]
    first, second = weight * left, weight * right
    spill = jnp.zeros_like(left)
    for j in range(1, taps):
        weight = columns[:, j : j + 1]
        moved_left = weight * pltpu.roll(left, j, 1)
        moved_right = weight * pltpu.roll(right, j, 1)
        head = lane < j
        first = first + jnp.where(head, 0.0, moved_left)
        second = second + jnp.where(head, moved_left, moved_right)
        spill = spill + jnp.where(head, moved_right, 0.0)
    return first, second, spill


def pack_kernel(key_ref, value_ref, filter_ref, weight_ref, out_ref, cols, product, extra, taken):
    taps = weight_ref.shape[1]
    rim = taps - 1
    channels = key_ref.shape[0]
    shards = out_ref.shape[0] // 17
    per = channels // shards
    for h in range(2):
        taken[h] = filter_ref[:, h * LANES : (h + 1) * LANES]
    for c in range(per):
        for h in range(2):
            out_ref[pl.ds(8 + h * 4 + c, shards, stride=17), :] = taken[
                h, pl.ds(c, shards, stride=per), :
            ]
    cols[0] = tap_columns(weight_ref[1])
    cols[1] = tap_columns(weight_ref[2])

    def body(m, carry):
        rows = pl.ds(pl.multiple_of(m * 8, 8), 8)
        k_first, k_second, k_spill = taps_of_rows(
            key_ref[rows, :LANES], key_ref[rows, LANES:], cols[0, rows, :], taps
        )
        v_first, v_second, v_spill = taps_of_rows(
            value_ref[rows, :LANES], value_ref[rows, LANES:], cols[1, rows, :], taps
        )
        lane = lax.broadcasted_iota(jnp.int32, k_first.shape, 1)
        product[0, rows, :] = jnp.where(lane < rim, k_first, k_first * v_first)
        product[1, rows, :] = k_second * v_second
        extra[rows, :] = (
            jnp.where(lane < rim, v_first, 0.0)
            + pltpu.roll(k_spill, rim, 1)
            + pltpu.roll(v_spill, 2 * rim, 1)
        )
        return carry

    lax.fori_loop(0, channels // 8, body, 0, unroll=4)
    line = extra[pl.ds(0, shards, stride=per), :]
    for c in range(1, per):
        line = line + pltpu.roll(extra[pl.ds(c, shards, stride=per), :], 32 * c, 1)
    out_ref[pl.ds(16, shards, stride=17), :] = line
    for c in range(per):
        for h in range(2):
            out_ref[pl.ds(h * 4 + c, shards, stride=17), :] = product[
                h, pl.ds(c, shards, stride=per), :
            ]


def query_kernel(query_ref, weight_ref, out_ref, spill_ref, cols, spilled):
    taps = weight_ref.shape[1]
    channels = query_ref.shape[0]
    cols[...] = tap_columns(weight_ref[0])

    def body(m, carry):
        rows = pl.ds(pl.multiple_of(m * 8, 8), 8)
        first, second, spill = taps_of_rows(
            query_ref[rows, :LANES], query_ref[rows, LANES:], cols[rows, :], taps
        )
        out_ref[rows, :LANES] = first
        out_ref[rows, LANES:] = second
        spilled[rows, :] = spill
        return carry

    lax.fori_loop(0, channels // 8, body, 0, unroll=4)
    spill_ref[...] = spilled[...].T[:8]


def conv_kernel(
    skip_ref, in_ref, rows_in, rows_out, turn, dft_high, dft_low, out_ref, zh, zl, gated, spec
):
    shards = in_ref.shape[0] // 17
    per = skip_ref.shape[0]
    rim = 6
    width = 2 * LANES
    lane = lax.broadcasted_iota(jnp.int32, (shards, LANES), 1)
    block = lax.broadcasted_iota(jnp.int32, (shards, LANES), 0)
    line = in_ref[pl.ds(16, shards, stride=17), :]
    prior = jnp.where(block == 0, 0.0, pltpu.roll(line, 1, 0))
    for c in range(per):
        here = pltpu.roll(line, (LANES - 32 * c) % LANES, 1) if c else line
        key_spill = pltpu.roll(prior, LANES - 32 * c - rim, 1)
        value_spill = pltpu.roll(prior, LANES - 32 * c - 2 * rim, 1)
        first = in_ref[pl.ds(c, shards, stride=17), :]
        first = jnp.where(lane < rim, (first + key_spill) * (here + value_spill), first)
        gated[c] = jnp.concatenate([first, in_ref[pl.ds(4 + c, shards, stride=17), :]], axis=1)
        taken = jnp.concatenate(
            [in_ref[pl.ds(8 + h * 4 + c, shards, stride=17), :] for h in range(2)], axis=1
        )
        for a, signal in enumerate((gated[c], taken)):
            high, low = split(signal)
            both = jnp.dot(
                rows_in[...],
                jnp.concatenate([high, low, high], axis=0),
                preferred_element_type=F32,
            )
            cos_part, sin_part = both[:shards], both[shards:]
            rows = pl.ds((a * per + c) * shards, shards)
            high, low = split(cos_part * turn[0] - sin_part * turn[1])
            zh[0, rows, :] = high
            zl[0, rows, :] = low
            high, low = split(cos_part * turn[1] + sin_part * turn[0])
            zh[1, rows, :] = high
            zl[1, rows, :] = low

    def times(lhs_high, lhs_low, which):
        return (
            jnp.dot(lhs_high, dft_high[which], preferred_element_type=F32)
            + jnp.dot(lhs_low, dft_high[which], preferred_element_type=F32)
            + jnp.dot(lhs_high, dft_low[which], preferred_element_type=F32)
        )

    spec[0] = times(zh[0], zl[0], 0) + times(zh[1], zl[1], 2)
    spec[1] = times(zh[0], zl[0], 1) + times(zh[1], zl[1], 0)
    count = per * shards
    sig_r, sig_i = spec[0, :count], spec[1, :count]
    fil_r, fil_i = spec[0, count:], spec[1, count:]
    real_high, real_low = split(sig_r * fil_r - sig_i * fil_i)
    imag_high, imag_low = split(sig_r * fil_i + sig_i * fil_r)
    back_r = times(real_high, real_low, 0) + times(imag_high, imag_low, 1)
    back_i = times(imag_high, imag_low, 0) + times(real_high, real_low, 2)
    spec[0, :count] = back_r
    spec[1, :count] = back_i
    for c in range(per):
        rows = pl.ds(c * shards, shards)
        br, bi = spec[0, rows, :], spec[1, rows, :]
        high, low = split(
            jnp.concatenate([br * turn[0] + bi * turn[1], bi * turn[0] - br * turn[1]], axis=0)
        )
        result = jnp.dot(
            rows_out[...], jnp.concatenate([high, low, high], axis=0), preferred_element_type=F32
        )
        result = result + skip_ref[c] * gated[c]
        for h in range(2):
            out_ref[pl.ds(h * 4 + c, shards, stride=8), :] = result[:, h * LANES : (h + 1) * LANES]


def gate_kernel(query_ref, spill_ref, conv_ref, out_ref):
    channels = query_ref.shape[0]
    padded = jnp.concatenate([spill_ref[...], jnp.zeros((LANES - 8, channels), F32)], axis=0)
    spill = padded.T
    for m in range(channels // 8):
        rows = slice(m * 8, m * 8 + 8)
        one, two = conv_ref[m * 16 : m * 16 + 8, :], conv_ref[m * 16 + 8 : m * 16 + 16, :]
        left = jnp.concatenate([one[:4], two[:4]], axis=0)
        right = jnp.concatenate([one[4:], two[4:]], axis=0)
        out_ref[rows, :LANES] = (query_ref[rows, :LANES] + spill[rows]) * left
        out_ref[rows, LANES:] = query_ref[rows, LANES:] * right


def on_device(query_in, key_in, value_in, short_weight, long_filter, skip_weight):
    channels, width = query_in.shape
    shards = lax.axis_size("ctx")
    per = channels // shards
    packed = pl.pallas_call(
        pack_kernel,
        out_shape=jax.ShapeDtypeStruct((shards * 17, LANES), F32),
        in_specs=[VMEM] * 4,
        out_specs=VMEM,
        scratch_shapes=[
            pltpu.VMEM((2, channels, LANES), F32),
            pltpu.VMEM((2, channels, LANES), F32),
            pltpu.VMEM((channels, LANES), F32),
            pltpu.VMEM((2, channels, LANES), F32),
        ],
        name="pack",
    )(key_in, value_in, long_filter, short_weight)
    moved = lax.all_to_all(
        packed.reshape(shards, 1, 17 * LANES), "ctx", split_axis=0, concat_axis=0, tiled=True
    ).reshape(shards * 17, LANES)
    query, spill = pl.pallas_call(
        query_kernel,
        out_shape=(
            jax.ShapeDtypeStruct((channels, width), F32),
            jax.ShapeDtypeStruct((8, channels), F32),
        ),
        in_specs=[VMEM] * 2,
        out_specs=(VMEM, VMEM),
        scratch_shapes=[pltpu.VMEM((channels, LANES), F32), pltpu.VMEM((channels, LANES), F32)],
        name="query",
    )(query_in, short_weight)
    spill = lax.ppermute(spill, "ctx", [(i, i + 1) for i in range(shards - 1)])
    skip = lax.dynamic_slice(skip_weight, (lax.axis_index("ctx") * per,), (per,))
    constants = [jnp.asarray(t) for t in tables(shards, width)]
    convolved = pl.pallas_call(
        conv_kernel,
        out_shape=jax.ShapeDtypeStruct((shards * 8, LANES), F32),
        in_specs=[SMEM] + [VMEM] * 6,
        out_specs=VMEM,
        scratch_shapes=[
            pltpu.VMEM((2, 2 * channels, width), BF16),
            pltpu.VMEM((2, 2 * channels, width), BF16),
            pltpu.VMEM((per, shards, width), F32),
            pltpu.VMEM((2, 2 * channels, width), F32),
        ],
        compiler_params=pltpu.CompilerParams(vmem_limit_bytes=24 * 1024 * 1024),
        name="conv",
    )(skip, moved, *constants)
    returned = lax.all_to_all(
        convolved.reshape(shards, 8, LANES), "ctx", split_axis=0, concat_axis=0, tiled=True
    ).reshape(shards * 8, LANES)
    return pl.pallas_call(
        gate_kernel,
        out_shape=jax.ShapeDtypeStruct((channels, width), F32),
        in_specs=[VMEM] * 3,
        out_specs=VMEM,
        name="gate",
    )(query, spill, returned)


def solution(mesh):
    return jax.shard_map(
        on_device,
        mesh=mesh,
        in_specs=(
            P("grp", "ctx"),
            P("grp", "ctx"),
            P("grp", "ctx"),
            P(None, None, "grp"),
            P("grp", "ctx"),
            P("grp"),
        ),
        out_specs=P("grp", "ctx"),
        check_vma=False,
    )
```

time: 208 us -> 68.6 us (0.33)
  the two profiles are of different devices: /device:TPU:33 before, /device:TPU:40 now
where the time goes in v1:
time: 68.6 us; the launch traced here: 68.3 us
  waiting for transfers between devices  31.1 us (45%)
  starting transfers between devices  21.7 us (32%)
  Pallas kernels  14 us (20%)
  local copies, waits for them, and re-layouts  1.47 us (2%)
    all_to_all x1, waiting for transfers between devices, on_device(): lax.all_to_all(packed.reshape(shards, 1, 17 * LANES), 'ctx', split_axis=0...  21 us
    all_to_all x1, starting transfers between devices, on_device(): lax.all_to_all(packed.reshape(shards, 1, 17 * LANES), 'ctx', split_axis=0...  13.8 us
    ppermute x1, waiting for transfers between devices, on_device(): spill = lax.ppermute(spill, 'ctx', [(i, i + 1) for i in range(shards - 1)])  10 us
    all_to_all x1, starting transfers between devices, on_device(): lax.all_to_all(convolved.reshape(shards, 8, LANES), 'ctx', split_axis=0,...  5.86 us
    pallas_call x1, Pallas kernels, on_device(): pl.pallas_call(pack_kernel, out_shape=jax.ShapeDtypeStruct((shards * 17,...  5.6 us
    pallas_call x1, Pallas kernels, on_device(): pl.pallas_call(conv_kernel, out_shape=jax.ShapeDtypeStruct((shards * 8, L...  3.3 us
    pallas_call x1, Pallas kernels, on_device(): pl.pallas_call(query_kernel, out_shape=(jax.ShapeDtypeStruct((channels, w...  3.2 us
    ppermute x1, starting transfers between devices, on_device(): spill = lax.ppermute(spill, 'ctx', [(i, i + 1) for i in range(shards - 1)])  2.04 us
  transfers between devices with their start and end apart: 3, of which 2 were waited for; matrix products, arithmetic and copies ran while one was open for 0% of the time, Pallas kernels for 5%

profile of v1, /device:TPU:40, one launch (start us, length us, event | category | flops | bytes accessed | tf_op | source)
XLA Modules:
  0.0 68.3 jit_solution(3499064596021943909)
XLA Ops:
  0.0 5.6 %pack.1 = f32[1088,128]{1,0:T(8,128)} custom-call(f32[256,256]{1,0:T(8,128)} %key_ref.1, f32[256,256]{1,0:T(8,128)} %value_ref.1, f32[256,256]{1,0:T(8,128)} %filter_ref.1, f32[3,7,256]{2,1,0:T(8,128)} %weight_ref.3), custom_call_target="tpu_custom_call" | custom-call | tf_op jit(solution)/shard_map/pack/pallas_call | solution.py:225
  5.6 0.0 copy-start
  5.6 0.0 copy-start.1
  5.6 0.0 copy-start.2
  5.6 0.0 copy-start.3
  5.6 0.0 copy-start.4
  5.6 13.8 %all-to-all-start = ((f32[64,1,2176]{2,1,0:T(1,128)}), f32[64,1,2176]{2,1,0:T(1,128)S(1)}, u32[]{:S(2)}, u32[]{:S(2)}) async-start(f32[64,1,2176]{2,1,0:T(1,128)} %bitcast.5), calls=%async_computation | async-start | bytes 1114112 | tf_op jit(solution)/shard_map/all_to_all | solution.py:238
  19.5 0.0 copy-start.7
  19.5 0.7 copy-done.7
  20.1 0.1 dynamic_slice.3.skip_ref
  20.2 21.0 %all-to-all-done = f32[64,1,2176]{2,1,0:T(1,128)S(1)} async-done(((f32[64,1,2176]{2,1,0:T(1,128)}), f32[64,1,2176]{2,1,0:T(1,128)S(1)}, u32[]{:S(2)}, u32[]{:S(2)}) %all-to-all-start) | async-done | bytes 557088 | tf_op jit(solution)/shard_map/all_to_all | solution.py:238
  41.2 0.0 copy-done
  41.2 0.0 copy-done.1
  41.2 0.0 copy-done.2
  41.2 0.0 copy-done.3
  41.2 0.0 copy-done.4
  41.3 3.3 %conv.1 = f32[512,128]{1,0:T(8,128)} custom-call(f32[4]{0:T(128)S(1)} %dynamic_slice.3.skip_ref, f32[1088,128]{1,0:T(8,128)S(1)} %bitcast.4, bf16[128,192]{1,0:T(8,128)(2,1)S(1)} %copy-done.3, bf16[64,384]{1,0:T(8,128)(2,1)S(1)} %copy-done.4, f32[2,64,256]{2,1,0:T(8,128)S(1)} %copy-done.2, bf16[3,256,256]{2,1,0:T(8,128)(2,1)S(1)} %copy-done, ...), custom_call_target="tpu_custom_call" | custom-call | tf_op jit(solution)/shard_map/conv/pallas_call | solution.py:255
  44.6 5.9 %all-to-all-start.1 = ((f32[64,8,128]{2,1,0:T(8,128)}), f32[64,8,128]{2,1,0:T(8,128)S(1)}, u32[]{:S(2)}, u32[]{:S(2)}) async-start(f32[64,8,128]{2,1,0:T(8,128)} %bitcast.2), calls=%async_computation.1 | async-start | bytes 524288 | tf_op jit(solution)/shard_map/all_to_all | solution.py:269
  50.4 3.2 %query.1 = (f32[256,256]{1,0:T(8,128)}, f32[8,256]{1,0:T(8,128)}) custom-call(f32[256,256]{1,0:T(8,128)} %query_ref.1, f32[3,7,256]{2,1,0:T(8,128)} %weight_ref.3), custom_call_target="tpu_custom_call" | custom-call | tf_op jit(solution)/shard_map/query/pallas_call | solution.py:241
  53.6 2.0 %collective-permute-start = (f32[8,256]{1,0:T(8,128)}, f32[8,256]{1,0:T(8,128)S(1)}, u32[]{:S(2)}, u32[]{:S(2)}) collective-permute-start(f32[8,256]{1,0:T(8,128)} %get-tuple-element.8), channel_id=1, source_target_pairs={{0,4},{4,8},{8,12},{12,16},{16,20},{20,24},{24,28},{28,32},{32,36}... | collective-permute-start | bytes 24584 | tf_op jit(solution)/shard_map/ppermute | solution.py:252
  55.7 10.0 %collective-permute-done.spill_ref = f32[8,256]{1,0:T(8,128)S(1)} collective-permute-done((f32[8,256]{1,0:T(8,128)}, f32[8,256]{1,0:T(8,128)S(1)}, u32[]{:S(2)}, u32[]{:S(2)}) %collective-permute-start) | collective-permute-done | bytes 8224 | tf_op jit(solution)/shard_map/ppermute | solution.py:252
  65.7 0.0 copy-start.6
  65.7 0.0 all-to-all-done.1
  65.7 0.0 copy-start.5
  65.7 0.6 copy-done.6
  66.3 0.1 copy-done.5
  66.4 1.9 %gate.1 = f32[256,256]{1,0:T(8,128)} custom-call(f32[256,256]{1,0:T(8,128)} %get-tuple-element.7.query_ref, f32[8,256]{1,0:T(8,128)} %copy-done.6, f32[512,128]{1,0:T(8,128)} %bitcast.6), custom_call_target="tpu_custom_call" | custom-call | tf_op jit(solution)/shard_map/gate/pallas_call | solution.py:272
Async XLA Ops:
  5.6 35.6 %copy-start = (bf16[3,256,256]{2,1,0:T(8,128)(2,1)S(1)}, bf16[3,256,256]{2,1,0:T(8,128)(2,1)}, u32[]{:S(2)}) copy-start(bf16[3,256,256]{2,1,0:T(8,128)(2,1)} %constant.25.clone.dft_high) | copy-start | bytes 1179652
  5.6 35.6 %copy-start.1 = (bf16[3,256,256]{2,1,0:T(8,128)(2,1)S(1)}, bf16[3,256,256]{2,1,0:T(8,128)(2,1)}, u32[]{:S(2)}) copy-start(bf16[3,256,256]{2,1,0:T(8,128)(2,1)} %constant.26.clone.dft_low) | copy-start | bytes 1179652
  5.6 35.6 %copy-start.2 = (f32[2,64,256]{2,1,0:T(8,128)S(1)}, f32[2,64,256]{2,1,0:T(8,128)}, u32[]{:S(2)}) copy-start(f32[2,64,256]{2,1,0:T(8,128)} %constant.24.clone.turn) | copy-start | bytes 393220
  5.6 35.6 %copy-start.3 = (bf16[128,192]{1,0:T(8,128)(2,1)S(1)}, bf16[128,192]{1,0:T(8,128)(2,1)}, u32[]{:S(2)}) copy-start(bf16[128,192]{1,0:T(8,128)(2,1)} %constant.22.clone.rows_in) | copy-start | bytes 147460
  5.6 35.6 %copy-start.4 = (bf16[64,384]{1,0:T(8,128)(2,1)S(1)}, bf16[64,384]{1,0:T(8,128)(2,1)}, u32[]{:S(2)}) copy-start(bf16[64,384]{1,0:T(8,128)(2,1)} %constant.23.clone.rows_out) | copy-start | bytes 147460
  5.6 35.6 %all-to-all-start = ((f32[64,1,2176]{2,1,0:T(1,128)}), f32[64,1,2176]{2,1,0:T(1,128)S(1)}, u32[]{:S(2)}, u32[]{:S(2)}) async-start(f32[64,1,2176]{2,1,0:T(1,128)} %bitcast.5), calls=%async_computation | async-start | bytes 1114112 | tf_op jit(solution)/shard_map/all_to_all | solution.py:238
  19.5 0.7 copy-start.7
  44.6 21.2 %all-to-all-start.1 = ((f32[64,8,128]{2,1,0:T(8,128)}), f32[64,8,128]{2,1,0:T(8,128)S(1)}, u32[]{:S(2)}, u32[]{:S(2)}) async-start(f32[64,8,128]{2,1,0:T(8,128)} %bitcast.2), calls=%async_computation.1 | async-start | bytes 524288 | tf_op jit(solution)/shard_map/all_to_all | solution.py:269
  53.6 12.1 %collective-permute-start = (f32[8,256]{1,0:T(8,128)}, f32[8,256]{1,0:T(8,128)S(1)}, u32[]{:S(2)}, u32[]{:S(2)}) collective-permute-start(f32[8,256]{1,0:T(8,128)} %get-tuple-element.8), channel_id=1, source_target_pairs={{0,4},{4,8},{8,12},{12,16},{16,20},{20,24},{24,28},{28,32},{32,36}... | collective-permute-start | bytes 24584 | tf_op jit(solution)/shard_map/ppermute | solution.py:252
  65.7 0.6 copy-start.6
  65.7 0.7 %copy-start.5 = (f32[64,8,128]{2,1,0:T(8,128)}, f32[64,8,128]{2,1,0:T(8,128)S(1)}, u32[]{:S(2)}) copy-start(f32[64,8,128]{2,1,0:T(8,128)S(1)} %all-to-all-done.1) | copy-start | bytes 786436

commit v2 on v1

--- a/solution.py
+++ b/solution.py
@@ -49,32 +49,20 @@
     )
 
 
-def tap_columns(weights):
-    taps, channels = weights.shape
-    padded = jnp.concatenate([weights, jnp.zeros((LANES - taps, channels), F32)], axis=0)
-    return padded.T
-
-
-def taps_of_rows(left, right, columns, taps):
-    lane = lax.broadcasted_iota(jnp.int32, left.shape, 1)
-    weight = columns[:, 0:1]
-    first, second = weight * left, weight * right
-    spill = jnp.zeros_like(left)
-    for j in range(1, taps):
-        weight = columns[:, j : j + 1]
-        moved_left = weight * pltpu.roll(left, j, 1)
-        moved_right = weight * pltpu.roll(right, j, 1)
-        head = lane < j
-        first = first + jnp.where(head, 0.0, moved_left)
-        second = second + jnp.where(head, moved_left, moved_right)
-        spill = spill + jnp.where(head, moved_right, 0.0)
-    return first, second, spill
-
-
-def pack_kernel(key_ref, value_ref, filter_ref, weight_ref, out_ref, cols, product, extra, taken):
-    taps = weight_ref.shape[1]
-    rim = taps - 1
-    channels = key_ref.shape[0]
+def causal_taps_at(rows_ref, weight_ref, stream, half, start):
+    lanes = slice(half * LANES, (half + 1) * LANES)
+    total = weight_ref[stream, 0:1, lanes] * rows_ref[half, 8 + start : 16 + start, :]
+    for j in range(1, weight_ref.shape[1]):
+        moved = rows_ref[half, 8 + start - j : 16 + start - j, :]
+        total = total + weight_ref[stream, j : j + 1, lanes] * moved
+    return total
+
+
+def pack_kernel(
+    key_ref, value_ref, filter_ref, weight_ref, out_ref, key_rows, value_rows, product, extra, taken
+):
+    rim = weight_ref.shape[1] - 1
+    channels, width = key_ref.shape
     shards = out_ref.shape[0] // 17
     per = channels // shards
     for h in range(2):
@@ -84,28 +72,33 @@
             out_ref[pl.ds(8 + h * 4 + c, shards, stride=17), :] = taken[
                 h, pl.ds(c, shards, stride=per), :
             ]
-    cols[0] = tap_columns(weight_ref[1])
-    cols[1] = tap_columns(weight_ref[2])
-
-    def body(m, carry):
-        rows = pl.ds(pl.multiple_of(m * 8, 8), 8)
-        k_first, k_second, k_spill = taps_of_rows(
-            key_ref[rows, :LANES], key_ref[rows, LANES:], cols[0, rows, :], taps
-        )
-        v_first, v_second, v_spill = taps_of_rows(
-            value_ref[rows, :LANES], value_ref[rows, LANES:], cols[1, rows, :], taps
-        )
-        lane = lax.broadcasted_iota(jnp.int32, k_first.shape, 1)
-        product[0, rows, :] = jnp.where(lane < rim, k_first, k_first * v_first)
-        product[1, rows, :] = k_second * v_second
-        extra[rows, :] = (
-            jnp.where(lane < rim, v_first, 0.0)
-            + pltpu.roll(k_spill, rim, 1)
-            + pltpu.roll(v_spill, 2 * rim, 1)
-        )
-        return carry
-
-    lax.fori_loop(0, channels // 8, body, 0, unroll=4)
+    edge = jnp.zeros((8, LANES), F32)
+    row = lax.broadcasted_iota(jnp.int32, (8, LANES), 0)
+    for half in range(2):
+        mine = slice(half * LANES, (half + 1) * LANES)
+        for rows, source in ((key_rows, key_ref), (value_rows, value_ref)):
+            rows[half, :8, :] = edge
+            rows[half, 8 + width :, :] = edge
+            for h in range(2):
+                part = slice(h * LANES, (h + 1) * LANES)
+                rows[half, 8 + h * LANES : 8 + (h + 1) * LANES, :] = source[mine, part].T
+        for h in range(2):
+            parts = []
+            for t in range(h * LANES, (h + 1) * LANES, 8):
+                key = causal_taps_at(key_rows, weight_ref, 1, half, t)
+                value = causal_taps_at(value_rows, weight_ref, 2, half, t)
+                if t == 0:
+                    value_head = value
+                    parts.append(jnp.where(row < rim, key, key * value))
+                else:
+                    parts.append(key * value)
+            product[h, mine, :] = jnp.concatenate(parts, axis=0).T
+        key_spill = causal_taps_at(key_rows, weight_ref, 1, half, width)
+        value_spill = causal_taps_at(value_rows, weight_ref, 2, half, width)
+        ends = jnp.concatenate(
+            [value_head, key_spill, value_spill, jnp.zeros((LANES - 24, LANES), F32)], axis=0
+        )
+        extra[mine, :] = ends.T
     line = extra[pl.ds(0, shards, stride=per), :]
     for c in range(1, per):
         line = line + pltpu.roll(extra[pl.ds(c, shards, stride=per), :], 32 * c, 1)
@@ -117,23 +110,21 @@
             ]
 
 
-def query_kernel(query_ref, weight_ref, out_ref, spill_ref, cols, spilled):
-    taps = weight_ref.shape[1]
-    channels = query_ref.shape[0]
-    cols[...] = tap_columns(weight_ref[0])
-
-    def body(m, carry):
-        rows = pl.ds(pl.multiple_of(m * 8, 8), 8)
-        first, second, spill = taps_of_rows(
-            query_ref[rows, :LANES], query_ref[rows, LANES:], cols[rows, :], taps
-        )
-        out_ref[rows, :LANES] = first
-        out_ref[rows, LANES:] = second
-        spilled[rows, :] = spill
-        return carry
-
-    lax.fori_loop(0, channels // 8, body, 0, unroll=4)
-    spill_ref[...] = spilled[...].T[:8]
+def query_kernel(query_ref, rim_ref, weight_ref, out_ref, query_rows):
+    rim = rim_ref.shape[0]
+    width = query_ref.shape[1]
+    for half in range(2):
+        mine = slice(half * LANES, (half + 1) * LANES)
+        query_rows[half, 8 - rim : 8, :] = rim_ref[:, mine]
+        for h in range(2):
+            part = slice(h * LANES, (h + 1) * LANES)
+            query_rows[half, 8 + h * LANES : 8 + (h + 1) * LANES, :] = query_ref[mine, part].T
+        for h in range(2):
+            parts = [
+                causal_taps_at(query_rows, weight_ref, 0, half, t)
+                for t in range(h * LANES, (h + 1) * LANES, 8)
+            ]
+            out_ref[mine, h * LANES : (h + 1) * LANES] = jnp.concatenate(parts, axis=0).T
 
 
 def conv_kernel(
@@ -149,8 +140,8 @@
     prior = jnp.where(block == 0, 0.0, pltpu.roll(line, 1, 0))
     for c in range(per):
         here = pltpu.roll(line, (LANES - 32 * c) % LANES, 1) if c else line
-        key_spill = pltpu.roll(prior, LANES - 32 * c - rim, 1)
-        value_spill = pltpu.roll(prior, LANES - 32 * c - 2 * rim, 1)
+        key_spill = pltpu.roll(prior, LANES - 32 * c - 8, 1)
+        value_spill = pltpu.roll(prior, LANES - 32 * c - 16, 1)
         first = in_ref[pl.ds(c, shards, stride=17), :]
         first = jnp.where(lane < rim, (first + key_spill) * (here + value_spill), first)
         gated[c] = jnp.concatenate([first, in_ref[pl.ds(4 + c, shards, stride=17), :]], axis=1)
@@ -205,52 +196,59 @@
             out_ref[pl.ds(h * 4 + c, shards, stride=8), :] = result[:, h * LANES : (h + 1) * LANES]
 
 
-def gate_kernel(query_ref, spill_ref, conv_ref, out_ref):
-    channels = query_ref.shape[0]
-    padded = jnp.concatenate([spill_ref[...], jnp.zeros((LANES - 8, channels), F32)], axis=0)
-    spill = padded.T
-    for m in range(channels // 8):
+def gate_kernel(query_ref, conv_ref, out_ref):
+    for m in range(query_ref.shape[0] // 8):
         rows = slice(m * 8, m * 8 + 8)
         one, two = conv_ref[m * 16 : m * 16 + 8, :], conv_ref[m * 16 + 8 : m * 16 + 16, :]
         left = jnp.concatenate([one[:4], two[:4]], axis=0)
         right = jnp.concatenate([one[4:], two[4:]], axis=0)
-        out_ref[rows, :LANES] = (query_ref[rows, :LANES] + spill[rows]) * left
+        out_ref[rows, :LANES] = query_ref[rows, :LANES] * left
         out_ref[rows, LANES:] = query_ref[rows, LANES:] * right
+
+
+def limit(mebibytes):
+    return pltpu.CompilerParams(vmem_limit_bytes=mebibytes * 1024 * 1024)
 
 
 def on_device(query_in, key_in, value_in, short_weight, long_filter, skip_weight):
     channels, width = query_in.shape
+    rim = short_weight.shape[1] - 1
     shards = lax.axis_size("ctx")
     per = channels // shards
+    rows = pltpu.VMEM((2, width + 16, LANES), F32)
     packed = pl.pallas_call(
         pack_kernel,
         out_shape=jax.ShapeDtypeStruct((shards * 17, LANES), F32),
         in_specs=[VMEM] * 4,
         out_specs=VMEM,
         scratch_shapes=[
-            pltpu.VMEM((2, channels, LANES), F32),
+            rows,
+            rows,
             pltpu.VMEM((2, channels, LANES), F32),
             pltpu.VMEM((channels, LANES), F32),
             pltpu.VMEM((2, channels, LANES), F32),
         ],
+        compiler_params=limit(8),
         name="pack",
     )(key_in, value_in, long_filter, short_weight)
+    packed, query_in, short_weight = lax.optimization_barrier((packed, query_in, short_weight))
     moved = lax.all_to_all(
         packed.reshape(shards, 1, 17 * LANES), "ctx", split_axis=0, concat_axis=0, tiled=True
     ).reshape(shards * 17, LANES)
-    query, spill = pl.pallas_call(
+    before = lax.ppermute(
+        query_in[:, width - rim :].T, "ctx", [(i, i + 1) for i in range(shards - 1)]
+    )
+    query = pl.pallas_call(
         query_kernel,
-        out_shape=(
-            jax.ShapeDtypeStruct((channels, width), F32),
-            jax.ShapeDtypeStruct((8, channels), F32),
-        ),
-        in_specs=[VMEM] * 2,
-        out_specs=(VMEM, VMEM),
-        scratch_shapes=[pltpu.VMEM((channels, LANES), F32), pltpu.VMEM((channels, LANES), F32)],
+        out_shape=jax.ShapeDtypeStruct((channels, width), F32),
+        in_specs=[VMEM] * 3,
+        out_specs=VMEM,
+        scratch_shapes=[rows],
+        compiler_params=limit(8),
         name="query",
-    )(query_in, short_weight)
-    spill = lax.ppermute(spill, "ctx", [(i, i + 1) for i in range(shards - 1)])
+    )(query_in, before, short_weight)
     skip = lax.dynamic_slice(skip_weight, (lax.axis_index("ctx") * per,), (per,))
+    moved, query = lax.optimization_barrier((moved, query))
     constants = [jnp.asarray(t) for t in tables(shards, width)]
     convolved = pl.pallas_call(
         conv_kernel,
@@ -263,7 +261,7 @@
             pltpu.VMEM((per, shards, width), F32),
             pltpu.VMEM((2, 2 * channels, width), F32),
         ],
-        compiler_params=pltpu.CompilerParams(vmem_limit_bytes=24 * 1024 * 1024),
+        compiler_params=limit(16),
         name="conv",
     )(skip, moved, *constants)
     returned = lax.all_to_all(
@@ -272,10 +270,11 @@
     return pl.pallas_call(
         gate_kernel,
         out_shape=jax.ShapeDtypeStruct((channels, width), F32),
-        in_specs=[VMEM] * 3,
-        out_specs=VMEM,
+        in_specs=[VMEM] * 2,
+        out_specs=VMEM,
+        compiler_params=limit(8),
         name="gate",
-    )(query, spill, returned)
+    )(query, returned)
 
 
 def solution(mesh):

time: 68.6 us -> 63.7 us (0.929)
  the two profiles are of different devices: /device:TPU:40 before, /device:TPU:33 now
where the time goes in v2:
time: 63.7 us; the launch traced here: 63.3 us
  starting transfers between devices  21.6 us (34%)
  blocking collectives  17.7 us (28%)
  waiting for transfers between devices  15 us (24%)
  Pallas kernels  4.99 us (8%)
  local copies, waits for them, and re-layouts  3.84 us (6%)
    all_to_all x1, blocking collectives, on_device(): lax.all_to_all(convolved.reshape(shards, 8, LANES), 'ctx', split_axis=0,...  17.7 us
    all_to_all x1, starting transfers between devices, on_device(): lax.all_to_all(packed.reshape(shards, 1, 17 * LANES), 'ctx', split_axis=0...  14 us
    all_to_all x1, waiting for transfers between devices, on_device(): lax.all_to_all(packed.reshape(shards, 1, 17 * LANES), 'ctx', split_axis=0...  10.8 us
    ppermute x1, starting transfers between devices, on_device(): lax.ppermute(query_in[:, width - rim:].T, 'ctx', [(i, i + 1) for i in ran...  7.58 us
    ppermute x1, waiting for transfers between devices, on_device(): lax.ppermute(query_in[:, width - rim:].T, 'ctx', [(i, i + 1) for i in ran...  4.21 us
    unnamed x24, local copies, waits for them, and re-layouts  3.63 us
    pallas_call x1, Pallas kernels, on_device(): pl.pallas_call(conv_kernel, out_shape=jax.ShapeDtypeStruct((shards * 8, L...  2.6 us
    pallas_call x1, Pallas kernels, on_device(): pl.pallas_call(pack_kernel, out_shape=jax.ShapeDtypeStruct((shards * 17,...  1.38 us
  transfers between devices with their start and end apart: 2, of which 2 were waited for; matrix products, arithmetic and copies ran while one was open for 0% of the time, Pallas kernels for 0%

profile of v2, /device:TPU:33, one launch (start us, length us, event | category | flops | bytes accessed | tf_op | source)
XLA Modules:
  0.0 63.3 jit_solution(6106219920554371155)
XLA Ops:
  0.0 0.0 copy-start.3
  0.0 0.9 %copy-done.3 = f32[256,256]{1,0:T(8,128)S(1)} copy-done((f32[256,256]{1,0:T(8,128)S(1)}, f32[256,256]{1,0:T(8,128)}, u32[]{:S(2)}) %copy-start.3) | copy-done | bytes 262168
  1.0 0.0 copy-start.4
  1.0 0.9 %copy-done.4 = f32[256,256]{1,0:T(8,128)S(1)} copy-done((f32[256,256]{1,0:T(8,128)S(1)}, f32[256,256]{1,0:T(8,128)}, u32[]{:S(2)}) %copy-start.4) | copy-done | bytes 262168
  1.9 0.0 copy-start.5
  1.9 0.9 %copy-done.5 = f32[256,256]{1,0:T(8,128)S(1)} copy-done((f32[256,256]{1,0:T(8,128)S(1)}, f32[256,256]{1,0:T(8,128)}, u32[]{:S(2)}) %copy-start.5) | copy-done | bytes 262168
  2.9 0.0 copy-start.7
  2.9 0.7 %copy-done.7 = f32[3,7,256]{2,1,0:T(8,128)S(1)} copy-done((f32[3,7,256]{2,1,0:T(8,128)S(1)}, f32[3,7,256]{2,1,0:T(8,128)}, u32[]{:S(2)}) %copy-start.7) | copy-done | bytes 21528
  3.6 1.4 %pack.1 = f32[1088,128]{1,0:T(8,128)} custom-call(f32[256,256]{1,0:T(8,128)S(1)} %copy-done.3, f32[256,256]{1,0:T(8,128)S(1)} %copy-done.4, f32[256,256]{1,0:T(8,128)S(1)} %copy-done.5, f32[3,7,256]{2,1,0:T(8,128)S(1)} %copy-done.7), custom_call_target="tpu_custom_call" | custom-call | tf_op jit(solution)/shard_map/pack/pallas_call | solution.py:219
  5.0 0.0 copy-start
  5.0 14.0 %all-to-all-start = ((f32[64,1,2176]{2,1,0:T(1,128)}), f32[64,1,2176]{2,1,0:T(1,128)S(1)}, u32[]{:S(2)}, u32[]{:S(2)}) async-start(f32[64,1,2176]{2,1,0:T(1,128)} %bitcast), calls=%async_computation | async-start | bytes 1114112 | tf_op jit(solution)/shard_map/all_to_all | solution.py:235
  19.0 0.0 copy-done
  19.0 0.0 copy-start.11
  19.0 0.0 copy-start.8
  19.0 0.0 copy-start.2
  19.0 0.0 copy-start.10
  19.1 0.1 copy.14
  19.2 0.0 copy-start.1
  19.2 7.6 %collective-permute-start = (f32[6,256]{1,0:T(8,128)S(1)}, f32[6,256]{1,0:T(8,128)S(1)}, u32[]{:S(2)}, u32[]{:S(2)}) collective-permute-start(f32[6,256]{1,0:T(8,128)S(1)} %slice_bitcast_fusion), channel_id=1, source_target_pairs={{0,4},{4,8},{8,12},{12,16},{16,20},{20,24},{24,28},{28,32},{32,36}... | collective-permute-start | bytes 18440 | tf_op jit(solution)/shard_map/ppermute | solution.py:238
  26.8 0.0 copy-done.11
  26.8 0.1 dynamic_slice.3.skip_ref
  26.9 0.0 copy-start.6
  26.9 0.0 copy-start.9
  26.9 4.2 %collective-permute-done.rim_ref = f32[6,256]{1,0:T(8,128)S(1)} collective-permute-done((f32[6,256]{1,0:T(8,128)S(1)}, f32[6,256]{1,0:T(8,128)S(1)}, u32[]{:S(2)}, u32[]{:S(2)}) %collective-permute-start) | collective-permute-done | bytes 6176 | tf_op jit(solution)/shard_map/ppermute | solution.py:238
  31.1 0.0 copy-done.8
  31.1 0.3 query.1.query_ref
  31.4 10.8 %all-to-all-done = f32[64,1,2176]{2,1,0:T(1,128)S(1)} async-done(((f32[64,1,2176]{2,1,0:T(1,128)}), f32[64,1,2176]{2,1,0:T(1,128)S(1)}, u32[]{:S(2)}, u32[]{:S(2)}) %all-to-all-start) | async-done | bytes 557088 | tf_op jit(solution)/shard_map/all_to_all | solution.py:235
  42.2 0.0 copy-done.2
  42.2 0.0 copy-done.10
  42.2 0.0 copy-done.1
  42.2 0.0 copy-done.6
  42.2 0.0 copy-done.9
  42.2 2.6 %conv.1 = f32[512,128]{1,0:T(8,128)S(1)} custom-call(f32[4]{0:T(128)S(1)} %dynamic_slice.3.skip_ref, f32[1088,128]{1,0:T(8,128)S(1)} %bitcast.6, bf16[128,192]{1,0:T(8,128)(2,1)S(1)} %copy-done.9, bf16[64,384]{1,0:T(8,128)(2,1)S(1)} %copy-done.10, f32[2,64,256]{2,1,0:T(8,128)S(1)} %copy-done.6, bf16[3,256,256]{2,1,0:T(8,128)(2,1)S(1)} %copy-done.1, ...), custom_call_target="tpu_custom_call" | custom-call | tf_op jit(solution)/shard_map/conv/pallas_call | solution.py:253
  44.8 17.7 %all_to_all.10 = f32[64,8,128]{2,1,0:T(8,128)S(1)} all-to-all(f32[64,8,128]{2,1,0:T(8,128)S(1)} %bitcast.8), channel_id=1, replica_groups=mesh['ctx'=64,'grp'=4] {'ctx'}, dimensions={0} | all-to-all | bytes 524288 | tf_op jit(solution)/shard_map/all_to_all | solution.py:267
  62.6 0.7 %gate.1 = f32[256,256]{1,0:T(8,128)} custom-call(f32[256,256]{1,0:T(8,128)S(1)} %query.1.query_ref, f32[512,128]{1,0:T(8,128)S(1)} %bitcast.7), custom_call_target="tpu_custom_call" | custom-call | tf_op jit(solution)/shard_map/gate/pallas_call | solution.py:270
  (1 shorter events, 0.0 us)
Async XLA Ops:
  0.0 0.9 %copy-start.3 = (f32[256,256]{1,0:T(8,128)S(1)}, f32[256,256]{1,0:T(8,128)}, u32[]{:S(2)}) copy-start(f32[256,256]{1,0:T(8,128)} %key_ref.1) | copy-start | bytes 786436
  1.0 0.9 %copy-start.4 = (f32[256,256]{1,0:T(8,128)S(1)}, f32[256,256]{1,0:T(8,128)}, u32[]{:S(2)}) copy-start(f32[256,256]{1,0:T(8,128)} %value_ref.1) | copy-start | bytes 786436
  1.9 0.9 %copy-start.5 = (f32[256,256]{1,0:T(8,128)S(1)}, f32[256,256]{1,0:T(8,128)}, u32[]{:S(2)}) copy-start(f32[256,256]{1,0:T(8,128)} %filter_ref.1) | copy-start | bytes 786436
  2.9 0.7 %copy-start.7 = (f32[3,7,256]{2,1,0:T(8,128)S(1)}, f32[3,7,256]{2,1,0:T(8,128)}, u32[]{:S(2)}) copy-start(f32[3,7,256]{2,1,0:T(8,128)} %weight_ref.2) | copy-start | bytes 64516
  5.0 14.0 %copy-start = (f32[256,256]{1,0:T(8,128)S(1)}, f32[256,256]{1,0:T(8,128)}, u32[]{:S(2)}) copy-start(f32[256,256]{1,0:T(8,128)} %query_ref) | copy-start | bytes 786436
  5.0 37.2 %all-to-all-start = ((f32[64,1,2176]{2,1,0:T(1,128)}), f32[64,1,2176]{2,1,0:T(1,128)S(1)}, u32[]{:S(2)}, u32[]{:S(2)}) async-start(f32[64,1,2176]{2,1,0:T(1,128)} %bitcast), calls=%async_computation | async-start | bytes 1114112 | tf_op jit(solution)/shard_map/all_to_all | solution.py:235
  19.0 7.8 %copy-start.11 = (f32[256]{0:T(256)S(1)}, f32[256]{0:T(256)}, u32[]{:S(2)}) copy-start(f32[256]{0:T(256)} %param.16) | copy-start | bytes 3076
  19.0 12.1 %copy-start.8 = (f32[3,7,256]{2,1,0:T(8,128)S(1)}, f32[3,7,256]{2,1,0:T(8,128)}, u32[]{:S(2)}) copy-start(f32[3,7,256]{2,1,0:T(8,128)} %weight_ref.2) | copy-start | bytes 64516
  19.0 23.2 %copy-start.2 = (bf16[3,256,256]{2,1,0:T(8,128)(2,1)S(1)}, bf16[3,256,256]{2,1,0:T(8,128)(2,1)}, u32[]{:S(2)}) copy-start(bf16[3,256,256]{2,1,0:T(8,128)(2,1)} %constant.26.clone.dft_low) | copy-start | bytes 1179652
  19.0 23.1 %copy-start.10 = (bf16[64,384]{1,0:T(8,128)(2,1)S(1)}, bf16[64,384]{1,0:T(8,128)(2,1)}, u32[]{:S(2)}) copy-start(bf16[64,384]{1,0:T(8,128)(2,1)} %constant.23.clone.rows_out) | copy-start | bytes 147460
  19.2 23.0 %copy-start.1 = (bf16[3,256,256]{2,1,0:T(8,128)(2,1)S(1)}, bf16[3,256,256]{2,1,0:T(8,128)(2,1)}, u32[]{:S(2)}) copy-start(bf16[3,256,256]{2,1,0:T(8,128)(2,1)} %constant.25.clone.dft_high) | copy-start | bytes 1179652
  19.2 11.9 %collective-permute-start = (f32[6,256]{1,0:T(8,128)S(1)}, f32[6,256]{1,0:T(8,128)S(1)}, u32[]{:S(2)}, u32[]{:S(2)}) collective-permute-start(f32[6,256]{1,0:T(8,128)S(1)} %slice_bitcast_fusion), channel_id=1, source_target_pairs={{0,4},{4,8},{8,12},{12,16},{16,20},{20,24},{24,28},{28,32},{32,36}... | collective-permute-start | bytes 18440 | tf_op jit(solution)/shard_map/ppermute | solution.py:238
  26.9 15.3 %copy-start.6 = (f32[2,64,256]{2,1,0:T(8,128)S(1)}, f32[2,64,256]{2,1,0:T(8,128)}, u32[]{:S(2)}) copy-start(f32[2,64,256]{2,1,0:T(8,128)} %constant.24.clone.turn) | copy-start | bytes 393220
  26.9 15.3 %copy-start.9 = (bf16[128,192]{1,0:T(8,128)(2,1)S(1)}, bf16[128,192]{1,0:T(8,128)(2,1)}, u32[]{:S(2)}) copy-start(bf16[128,192]{1,0:T(8,128)(2,1)} %constant.22.clone.rows_in) | copy-start | bytes 147460

commit v3 on v2

--- a/solution.py
+++ b/solution.py
@@ -13,6 +13,7 @@
 F32 = jnp.float32
 BF16 = jnp.bfloat16
 VMEM = pl.BlockSpec(memory_space=pltpu.VMEM)
+HBM = pl.BlockSpec(memory_space=pltpu.HBM)
 SMEM = pl.BlockSpec(memory_space=pltpu.SMEM)
 
 
@@ -59,26 +60,57 @@
 
 
 def pack_kernel(
-    key_ref, value_ref, filter_ref, weight_ref, out_ref, key_rows, value_rows, product, extra, taken
+    key_hbm,
+    value_hbm,
+    filter_hbm,
+    weight_hbm,
+    out_hbm,
+    key_ref,
+    value_ref,
+    filter_ref,
+    weight_ref,
+    out_ref,
+    key_rows,
+    value_rows,
+    product,
+    extra,
+    in_sem,
+    out_sem,
 ):
     rim = weight_ref.shape[1] - 1
     channels, width = key_ref.shape
-    shards = out_ref.shape[0] // 17
-    per = channels // shards
-    for h in range(2):
-        taken[h] = filter_ref[:, h * LANES : (h + 1) * LANES]
-    for c in range(per):
-        for h in range(2):
-            out_ref[pl.ds(8 + h * 4 + c, shards, stride=17), :] = taken[
-                h, pl.ds(c, shards, stride=per), :
-            ]
+    group = out_ref.shape[0] // 2
+    owners = group // 17
+    per = channels // (2 * owners)
+    arrivals = [pltpu.make_async_copy(weight_hbm, weight_ref, in_sem.at[0])]
+    for half in range(2):
+        mine = pl.ds(half * LANES, LANES)
+        for n, (source, target) in enumerate(((key_hbm, key_ref), (value_hbm, value_ref))):
+            arrivals.append(
+                pltpu.make_async_copy(
+                    source.at[mine, :], target.at[mine, :], in_sem.at[1 + 4 * half + n]
+                )
+            )
+        for h in range(2):
+            arrivals.append(
+                pltpu.make_async_copy(
+                    filter_hbm.at[mine, pl.ds(h * LANES, LANES)],
+                    filter_ref.at[h, mine, :],
+                    in_sem.at[3 + 4 * half + h],
+                )
+            )
+    for copy in arrivals:
+        copy.start()
     edge = jnp.zeros((8, LANES), F32)
     row = lax.broadcasted_iota(jnp.int32, (8, LANES), 0)
+    arrivals[0].wait()
+    departures = []
     for half in range(2):
         mine = slice(half * LANES, (half + 1) * LANES)
-        for rows, source in ((key_rows, key_ref), (value_rows, value_ref)):
+        for n, (rows, source) in enumerate(((key_rows, key_ref), (value_rows, value_ref))):
             rows[half, :8, :] = edge
             rows[half, 8 + width :, :] = edge
+            arrivals[1 + 4 * half + n].wait()
             for h in range(2):
                 part = slice(h * LANES, (h + 1) * LANES)
                 rows[half, 8 + h * LANES : 8 + (h + 1) * LANES, :] = source[mine, part].T
@@ -99,15 +131,26 @@
             [value_head, key_spill, value_spill, jnp.zeros((LANES - 24, LANES), F32)], axis=0
         )
         extra[mine, :] = ends.T
-    line = extra[pl.ds(0, shards, stride=per), :]
-    for c in range(1, per):
-        line = line + pltpu.roll(extra[pl.ds(c, shards, stride=per), :], 32 * c, 1)
-    out_ref[pl.ds(16, shards, stride=17), :] = line
-    for c in range(per):
-        for h in range(2):
-            out_ref[pl.ds(h * 4 + c, shards, stride=17), :] = product[
-                h, pl.ds(c, shards, stride=per), :
-            ]
+        arrivals[3 + 4 * half].wait()
+        arrivals[4 + 4 * half].wait()
+        start = half * group
+        line = extra[pl.ds(half * LANES, owners, stride=per), :]
+        for c in range(per):
+            own = pl.ds(half * LANES + c, owners, stride=per)
+            if c:
+                line = line + pltpu.roll(extra[own, :], 32 * c, 1)
+            for h in range(2):
+                r = start + h * 4 + c
+                out_ref[pl.ds(r, owners, stride=17), :] = product[h, own, :]
+                out_ref[pl.ds(8 + r, owners, stride=17), :] = filter_ref[h, own, :]
+        out_ref[pl.ds(start + 16, owners, stride=17), :] = line
+        copy = pltpu.make_async_copy(
+            out_ref.at[pl.ds(start, group), :], out_hbm.at[pl.ds(start, group), :], out_sem.at[half]
+        )
+        copy.start()
+        departures.append(copy)
+    for copy in departures:
+        copy.wait()
 
 
 def query_kernel(query_ref, rim_ref, weight_ref, out_ref, query_rows):
@@ -219,16 +262,22 @@
     packed = pl.pallas_call(
         pack_kernel,
         out_shape=jax.ShapeDtypeStruct((shards * 17, LANES), F32),
-        in_specs=[VMEM] * 4,
-        out_specs=VMEM,
+        in_specs=[HBM] * 4,
+        out_specs=HBM,
         scratch_shapes=[
+            pltpu.VMEM((channels, width), F32),
+            pltpu.VMEM((channels, width), F32),
+            pltpu.VMEM((2, channels, LANES), F32),
+            pltpu.VMEM(short_weight.shape, F32),
+            pltpu.VMEM((shards * 17, LANES), F32),
             rows,
             rows,
             pltpu.VMEM((2, channels, LANES), F32),
             pltpu.VMEM((channels, LANES), F32),
-            pltpu.VMEM((2, channels, LANES), F32),
+            pltpu.SemaphoreType.DMA((9,)),
+            pltpu.SemaphoreType.DMA((2,)),
         ],
-        compiler_params=limit(8),
+        compiler_params=limit(60),
         name="pack",
     )(key_in, value_in, long_filter, short_weight)
     packed, query_in, short_weight = lax.optimization_barrier((packed, query_in, short_weight))

time: 63.7 us -> 61.2 us (0.961)
  local copies, waits for them, and re-layouts: 3.84 us -> 0.26 us
  Pallas kernels: 4.99 us -> 6.19 us
    unnamed x24 -> x16, local copies, waits for them, and re-layouts: 3.63 us -> 0.05 us
    pallas_call x1, Pallas kernels: 1.38 us -> 2.57 us  [on_device(): pl.pallas_call(pack_kernel, out_shape=jax.ShapeDtypeStruct((shards * 17,...]
where the time goes in v3:
time: 61.2 us; the launch traced here: 60.9 us
  starting transfers between devices  21.6 us (35%)
  blocking collectives  17.7 us (29%)
  waiting for transfers between devices  15 us (25%)
  Pallas kernels  6.19 us (10%)
    all_to_all x1, blocking collectives, on_device(): lax.all_to_all(convolved.reshape(shards, 8, LANES), 'ctx', split_axis=0,...  17.7 us
    all_to_all x1, starting transfers between devices, on_device(): lax.all_to_all(packed.reshape(shards, 1, 17 * LANES), 'ctx', split_axis=0...  14 us
    all_to_all x1, waiting for transfers between devices, on_device(): lax.all_to_all(packed.reshape(shards, 1, 17 * LANES), 'ctx', split_axis=0...  10.8 us
    ppermute x1, starting transfers between devices, on_device(): lax.ppermute(query_in[:, width - rim:].T, 'ctx', [(i, i + 1) for i in ran...  7.58 us
    ppermute x1, waiting for transfers between devices, on_device(): lax.ppermute(query_in[:, width - rim:].T, 'ctx', [(i, i + 1) for i in ran...  4.21 us
    pallas_call x1, Pallas kernels, on_device(): pl.pallas_call(conv_kernel, out_shape=jax.ShapeDtypeStruct((shards * 8, L...  2.62 us
    pallas_call x1, Pallas kernels, on_device(): pl.pallas_call(pack_kernel, out_shape=jax.ShapeDtypeStruct((shards * 17,...  2.57 us
  transfers between devices with their start and end apart: 2, of which 2 were waited for; matrix products, arithmetic and copies ran while one was open for 0% of the time, Pallas kernels for 0%

profile of v3, /device:TPU:33, one launch (start us, length us, event | category | flops | bytes accessed | tf_op | source)
XLA Modules:
  0.0 60.9 jit_solution(18438364225619338926)
XLA Ops:
  0.0 2.6 %pack.1 = f32[1088,128]{1,0:T(8,128)} custom-call(f32[256,256]{1,0:T(8,128)} %key_hbm.1, f32[256,256]{1,0:T(8,128)} %value_hbm.1, f32[256,256]{1,0:T(8,128)} %filter_hbm.1, f32[3,7,256]{2,1,0:T(8,128)} %weight_ref), custom_call_target="tpu_custom_call" | custom-call | tf_op jit(solution)/shard_map/pack/pallas_call | solution.py:262
  2.6 0.0 copy-start
  2.6 14.0 %all-to-all-start = ((f32[64,1,2176]{2,1,0:T(1,128)}), f32[64,1,2176]{2,1,0:T(1,128)S(1)}, u32[]{:S(2)}, u32[]{:S(2)}) async-start(f32[64,1,2176]{2,1,0:T(1,128)} %bitcast.9), calls=%async_computation | async-start | bytes 1114112 | tf_op jit(solution)/shard_map/all_to_all | solution.py:284
  16.6 0.0 copy-done
  16.6 0.0 copy-start.7
  16.6 0.0 copy-start.4
  16.7 0.0 copy-start.2
  16.7 0.0 copy-start.6
  16.7 0.1 copy.14
  16.8 0.0 copy-start.1
  16.8 7.6 %collective-permute-start = (f32[6,256]{1,0:T(8,128)S(1)}, f32[6,256]{1,0:T(8,128)S(1)}, u32[]{:S(2)}, u32[]{:S(2)}) collective-permute-start(f32[6,256]{1,0:T(8,128)S(1)} %slice_bitcast_fusion), channel_id=1, source_target_pairs={{0,4},{4,8},{8,12},{12,16},{16,20},{20,24},{24,28},{28,32},{32,36}... | collective-permute-start | bytes 18440 | tf_op jit(solution)/shard_map/ppermute | solution.py:287
  24.4 0.0 copy-done.7
  24.4 0.1 dynamic_slice.3.skip_ref
  24.5 0.0 copy-start.3
  24.5 0.0 copy-start.5
  24.5 4.2 %collective-permute-done.rim_ref = f32[6,256]{1,0:T(8,128)S(1)} collective-permute-done((f32[6,256]{1,0:T(8,128)S(1)}, f32[6,256]{1,0:T(8,128)S(1)}, u32[]{:S(2)}, u32[]{:S(2)}) %collective-permute-start) | collective-permute-done | bytes 6176 | tf_op jit(solution)/shard_map/ppermute | solution.py:287
  28.7 0.0 copy-done.4
  28.7 0.3 query.1.query_ref
  29.0 10.8 %all-to-all-done = f32[64,1,2176]{2,1,0:T(1,128)S(1)} async-done(((f32[64,1,2176]{2,1,0:T(1,128)}), f32[64,1,2176]{2,1,0:T(1,128)S(1)}, u32[]{:S(2)}, u32[]{:S(2)}) %all-to-all-start) | async-done | bytes 557088 | tf_op jit(solution)/shard_map/all_to_all | solution.py:284
  39.8 0.0 copy-done.2
  39.8 0.0 copy-done.6
  39.8 0.0 copy-done.1
  39.8 0.0 copy-done.3
  39.8 0.0 copy-done.5
  39.8 2.6 %conv.1 = f32[512,128]{1,0:T(8,128)S(1)} custom-call(f32[4]{0:T(128)S(1)} %dynamic_slice.3.skip_ref, f32[1088,128]{1,0:T(8,128)S(1)} %bitcast.6, bf16[128,192]{1,0:T(8,128)(2,1)S(1)} %copy-done.5, bf16[64,384]{1,0:T(8,128)(2,1)S(1)} %copy-done.6, f32[2,64,256]{2,1,0:T(8,128)S(1)} %copy-done.3, bf16[3,256,256]{2,1,0:T(8,128)(2,1)S(1)} %copy-done.1, ...), custom_call_target="tpu_custom_call" | custom-call | tf_op jit(solution)/shard_map/conv/pallas_call | solution.py:302
  42.5 17.7 %all_to_all.10 = f32[64,8,128]{2,1,0:T(8,128)S(1)} all-to-all(f32[64,8,128]{2,1,0:T(8,128)S(1)} %bitcast.8), channel_id=1, replica_groups=mesh['ctx'=64,'grp'=4] {'ctx'}, dimensions={0} | all-to-all | bytes 524288 | tf_op jit(solution)/shard_map/all_to_all | solution.py:316
  60.2 0.7 %gate.1 = f32[256,256]{1,0:T(8,128)} custom-call(f32[256,256]{1,0:T(8,128)S(1)} %query.1.query_ref, f32[512,128]{1,0:T(8,128)S(1)} %bitcast.7), custom_call_target="tpu_custom_call" | custom-call | tf_op jit(solution)/shard_map/gate/pallas_call | solution.py:319
  (1 shorter events, 0.0 us)
Async XLA Ops:
  2.6 14.1 %copy-start = (f32[256,256]{1,0:T(8,128)S(1)}, f32[256,256]{1,0:T(8,128)}, u32[]{:S(2)}) copy-start(f32[256,256]{1,0:T(8,128)} %query_ref) | copy-start | bytes 786436
  2.6 37.2 %all-to-all-start = ((f32[64,1,2176]{2,1,0:T(1,128)}), f32[64,1,2176]{2,1,0:T(1,128)S(1)}, u32[]{:S(2)}, u32[]{:S(2)}) async-start(f32[64,1,2176]{2,1,0:T(1,128)} %bitcast.9), calls=%async_computation | async-start | bytes 1114112 | tf_op jit(solution)/shard_map/all_to_all | solution.py:284
  16.6 7.8 %copy-start.7 = (f32[256]{0:T(256)S(1)}, f32[256]{0:T(256)}, u32[]{:S(2)}) copy-start(f32[256]{0:T(256)} %param.16) | copy-start | bytes 3076
  16.6 12.1 %copy-start.4 = (f32[3,7,256]{2,1,0:T(8,128)S(1)}, f32[3,7,256]{2,1,0:T(8,128)}, u32[]{:S(2)}) copy-start(f32[3,7,256]{2,1,0:T(8,128)} %weight_ref) | copy-start | bytes 64516
  16.7 23.2 %copy-start.2 = (bf16[3,256,256]{2,1,0:T(8,128)(2,1)S(1)}, bf16[3,256,256]{2,1,0:T(8,128)(2,1)}, u32[]{:S(2)}) copy-start(bf16[3,256,256]{2,1,0:T(8,128)(2,1)} %constant.26.clone.dft_low) | copy-start | bytes 1179652
  16.7 23.1 %copy-start.6 = (bf16[64,384]{1,0:T(8,128)(2,1)S(1)}, bf16[64,384]{1,0:T(8,128)(2,1)}, u32[]{:S(2)}) copy-start(bf16[64,384]{1,0:T(8,128)(2,1)} %constant.23.clone.rows_out) | copy-start | bytes 147460
  16.8 23.0 %copy-start.1 = (bf16[3,256,256]{2,1,0:T(8,128)(2,1)S(1)}, bf16[3,256,256]{2,1,0:T(8,128)(2,1)}, u32[]{:S(2)}) copy-start(bf16[3,256,256]{2,1,0:T(8,128)(2,1)} %constant.25.clone.dft_high) | copy-start | bytes 1179652
  16.8 11.9 %collective-permute-start = (f32[6,256]{1,0:T(8,128)S(1)}, f32[6,256]{1,0:T(8,128)S(1)}, u32[]{:S(2)}, u32[]{:S(2)}) collective-permute-start(f32[6,256]{1,0:T(8,128)S(1)} %slice_bitcast_fusion), channel_id=1, source_target_pairs={{0,4},{4,8},{8,12},{12,16},{16,20},{20,24},{24,28},{28,32},{32,36}... | collective-permute-start | bytes 18440 | tf_op jit(solution)/shard_map/ppermute | solution.py:287
  24.5 15.3 %copy-start.3 = (f32[2,64,256]{2,1,0:T(8,128)S(1)}, f32[2,64,256]{2,1,0:T(8,128)}, u32[]{:S(2)}) copy-start(f32[2,64,256]{2,1,0:T(8,128)} %constant.24.clone.turn) | copy-start | bytes 393220
  24.5 15.3 %copy-start.5 = (bf16[128,192]{1,0:T(8,128)(2,1)S(1)}, bf16[128,192]{1,0:T(8,128)(2,1)}, u32[]{:S(2)}) copy-start(bf16[128,192]{1,0:T(8,128)(2,1)} %constant.22.clone.rows_in) | copy-start | bytes 147460

commit v4 on v3

--- a/solution.py
+++ b/solution.py
@@ -1,3 +1,4 @@
+import functools
 import math
 
 import jax
@@ -10,6 +11,7 @@
 from jax.sharding import PartitionSpec as P
 
 LANES = 128
+STEP = 128
 F32 = jnp.float32
 BF16 = jnp.bfloat16
 VMEM = pl.BlockSpec(memory_space=pltpu.VMEM)
@@ -38,15 +40,19 @@
     rows_out = np.concatenate([high, high, low], axis=1)
     order = 4 * blocks * width
     turn = 2.0 * math.pi * (odd[:, None] * np.arange(width)[None, :] % order) / order
-    index = np.arange(width)
-    phase = 2.0 * math.pi * (index[:, None] * index[None, :] % width) / width
-    high, low = halves(np.stack([np.cos(phase), np.sin(phase), -np.sin(phase)]))
+    half = width // 2
+    index = np.arange(half)
+    fold = 2.0 * math.pi * np.broadcast_to(index, (blocks, half)) / width
+    phase = 2.0 * math.pi * (index[:, None] * index[None, :] % half) / half
+    cos, sin = np.cos(phase), np.sin(phase)
+    forward = np.block([[cos, sin], [-sin, cos]])
+    high, low = halves(np.stack([forward, forward.T]))
     return (
         rows_in,
         rows_out,
         np.stack([np.cos(turn), np.sin(turn)]).astype(np.float32),
-        high,
-        low,
+        np.stack([np.cos(fold), np.sin(fold)]).astype(np.float32),
+        np.concatenate([high, high, low], axis=1),
     )
 
 
@@ -171,72 +177,94 @@
 
 
 def conv_kernel(
-    skip_ref, in_ref, rows_in, rows_out, turn, dft_high, dft_low, out_ref, zh, zl, gated, spec
+    rim, skip_ref, in_ref, rows_in, rows_out, turn, fold, dft, out_ref, gated, first_step, lhs, spec
 ):
     shards = in_ref.shape[0] // 17
     per = skip_ref.shape[0]
-    rim = 6
-    width = 2 * LANES
     lane = lax.broadcasted_iota(jnp.int32, (shards, LANES), 1)
     block = lax.broadcasted_iota(jnp.int32, (shards, LANES), 0)
     line = in_ref[pl.ds(16, shards, stride=17), :]
     prior = jnp.where(block == 0, 0.0, pltpu.roll(line, 1, 0))
+    left, right = slice(0, LANES), slice(LANES, 2 * LANES)
+
+    def triple(value):
+        top, rest = split(value)
+        return jnp.concatenate([top, rest, top], axis=0)
+
+    def put(rows, part, value):
+        top, rest = split(value)
+        for n, term in enumerate((top, rest, top)):
+            lhs[rows, pl.ds((2 * n + part) * LANES, LANES)] = term
+
+    signals = []
     for c in range(per):
         here = pltpu.roll(line, (LANES - 32 * c) % LANES, 1) if c else line
         key_spill = pltpu.roll(prior, LANES - 32 * c - 8, 1)
         value_spill = pltpu.roll(prior, LANES - 32 * c - 16, 1)
         first = in_ref[pl.ds(c, shards, stride=17), :]
         first = jnp.where(lane < rim, (first + key_spill) * (here + value_spill), first)
-        gated[c] = jnp.concatenate([first, in_ref[pl.ds(4 + c, shards, stride=17), :]], axis=1)
-        taken = jnp.concatenate(
-            [in_ref[pl.ds(8 + h * 4 + c, shards, stride=17), :] for h in range(2)], axis=1
-        )
-        for a, signal in enumerate((gated[c], taken)):
-            high, low = split(signal)
-            both = jnp.dot(
-                rows_in[...],
-                jnp.concatenate([high, low, high], axis=0),
-                preferred_element_type=F32,
+        second = in_ref[pl.ds(4 + c, shards, stride=17), :]
+        gated[c, :, left] = first
+        gated[c, :, right] = second
+        signals.append(jnp.concatenate([first, second], axis=1))
+    for c in range(per):
+        signals.append(
+            jnp.concatenate(
+                [in_ref[pl.ds(8 + h * 4 + c, shards, stride=17), :] for h in range(2)], axis=1
             )
-            cos_part, sin_part = both[:shards], both[shards:]
-            rows = pl.ds((a * per + c) * shards, shards)
-            high, low = split(cos_part * turn[0] - sin_part * turn[1])
-            zh[0, rows, :] = high
-            zl[0, rows, :] = low
-            high, low = split(cos_part * turn[1] + sin_part * turn[0])
-            zh[1, rows, :] = high
-            zl[1, rows, :] = low
-
-    def times(lhs_high, lhs_low, which):
-        return (
-            jnp.dot(lhs_high, dft_high[which], preferred_element_type=F32)
-            + jnp.dot(lhs_low, dft_high[which], preferred_element_type=F32)
-            + jnp.dot(lhs_high, dft_low[which], preferred_element_type=F32)
-        )
-
-    spec[0] = times(zh[0], zl[0], 0) + times(zh[1], zl[1], 2)
-    spec[1] = times(zh[0], zl[0], 1) + times(zh[1], zl[1], 0)
-    count = per * shards
-    sig_r, sig_i = spec[0, :count], spec[1, :count]
-    fil_r, fil_i = spec[0, count:], spec[1, count:]
-    real_high, real_low = split(sig_r * fil_r - sig_i * fil_i)
-    imag_high, imag_low = split(sig_r * fil_i + sig_i * fil_r)
-    back_r = times(real_high, real_low, 0) + times(imag_high, imag_low, 1)
-    back_i = times(imag_high, imag_low, 0) + times(real_high, real_low, 2)
-    spec[0, :count] = back_r
-    spec[1, :count] = back_i
+        )
+    for n, signal in enumerate(signals):
+        first_step[n] = jnp.dot(rows_in[...], triple(signal), preferred_element_type=F32)
+    count = 2 * per * shards
+    for n in range(2 * per):
+        a, c = divmod(n, per)
+        cos_part, sin_part = first_step[n, :shards, :], first_step[n, shards:, :]
+        real = cos_part * turn[0] - sin_part * turn[1]
+        imag = cos_part * turn[1] + sin_part * turn[0]
+        even = pl.ds(a * count + c * shards, shards)
+        odd = pl.ds(a * count + (per + c) * shards, shards)
+        put(even, 0, real[:, left] + real[:, right])
+        put(even, 1, imag[:, left] + imag[:, right])
+        real, imag = real[:, left] - real[:, right], imag[:, left] - imag[:, right]
+        put(odd, 0, real * fold[0] - imag * fold[1])
+        put(odd, 1, real * fold[1] + imag * fold[0])
+    for r in range(0, 2 * count, STEP):
+        spec[r : r + STEP] = jnp.dot(
+            lhs[r : r + STEP], dft[0], preferred_element_type=F32
+        )
+    for n in range(2 * per):
+        rows = pl.ds(n * shards, shards)
+        twin = pl.ds(count + n * shards, shards)
+        sig_r, sig_i = spec[rows, left], spec[rows, right]
+        fil_r, fil_i = spec[twin, left], spec[twin, right]
+        put(rows, 0, sig_r * fil_r - sig_i * fil_i)
+        put(rows, 1, sig_r * fil_i + sig_i * fil_r)
+    for r in range(0, count, STEP):
+        spec[r : r + STEP] = jnp.dot(
+            lhs[r : r + STEP], dft[1], preferred_element_type=F32
+        )
+    values = []
     for c in range(per):
-        rows = pl.ds(c * shards, shards)
-        br, bi = spec[0, rows, :], spec[1, rows, :]
-        high, low = split(
-            jnp.concatenate([br * turn[0] + bi * turn[1], bi * turn[0] - br * turn[1]], axis=0)
-        )
-        result = jnp.dot(
-            rows_out[...], jnp.concatenate([high, low, high], axis=0), preferred_element_type=F32
-        )
+        even = pl.ds(c * shards, shards)
+        odd = pl.ds((per + c) * shards, shards)
+        real, imag = spec[odd, left], spec[odd, right]
+        turned_r = real * fold[0] + imag * fold[1]
+        turned_i = imag * fold[0] - real * fold[1]
+        real, imag = spec[even, left], spec[even, right]
+        real = jnp.concatenate([real + turned_r, real - turned_r], axis=1)
+        imag = jnp.concatenate([imag + turned_i, imag - turned_i], axis=1)
+        values.append(
+            triple(
+                jnp.concatenate(
+                    [real * turn[0] + imag * turn[1], imag * turn[0] - real * turn[1]], axis=0
+                )
+            )
+        )
+    for c in range(per):
+        result = jnp.dot(rows_out[...], values[c], preferred_element_type=F32)
         result = result + skip_ref[c] * gated[c]
-        for h in range(2):
-            out_ref[pl.ds(h * 4 + c, shards, stride=8), :] = result[:, h * LANES : (h + 1) * LANES]
+        out_ref[pl.ds(c, shards, stride=8), :] = result[:, left]
+        out_ref[pl.ds(4 + c, shards, stride=8), :] = result[:, right]
 
 
 def gate_kernel(query_ref, conv_ref, out_ref):
@@ -300,15 +328,15 @@
     moved, query = lax.optimization_barrier((moved, query))
     constants = [jnp.asarray(t) for t in tables(shards, width)]
     convolved = pl.pallas_call(
-        conv_kernel,
+        functools.partial(conv_kernel, rim),
         out_shape=jax.ShapeDtypeStruct((shards * 8, LANES), F32),
         in_specs=[SMEM] + [VMEM] * 6,
         out_specs=VMEM,
         scratch_shapes=[
-            pltpu.VMEM((2, 2 * channels, width), BF16),
-            pltpu.VMEM((2, 2 * channels, width), BF16),
             pltpu.VMEM((per, shards, width), F32),
-            pltpu.VMEM((2, 2 * channels, width), F32),
+            pltpu.VMEM((2 * per, 2 * shards, width), F32),
+            pltpu.VMEM((4 * channels, 3 * width), BF16),
+            pltpu.VMEM((4 * channels, width), F32),
         ],
         compiler_params=limit(16),
         name="conv",

time: 61.2 us -> 60.7 us (level)
  no operation moved by 1% of the time
where the time goes in v4:
time: 60.7 us; the launch traced here: 60.4 us
  starting transfers between devices  21.6 us (36%)
  blocking collectives  17.7 us (29%)
  waiting for transfers between devices  15.1 us (25%)
  Pallas kernels  5.68 us (9%)
    all_to_all x1, blocking collectives, on_device(): lax.all_to_all(convolved.reshape(shards, 8, LANES), 'ctx', split_axis=0,...  17.7 us
    all_to_all x1, starting transfers between devices, on_device(): lax.all_to_all(packed.reshape(shards, 1, 17 * LANES), 'ctx', split_axis=0...  14 us
    all_to_all x1, waiting for transfers between devices, on_device(): lax.all_to_all(packed.reshape(shards, 1, 17 * LANES), 'ctx', split_axis=0...  10.8 us
    ppermute x1, starting transfers between devices, on_device(): lax.ppermute(query_in[:, width - rim:].T, 'ctx', [(i, i + 1) for i in ran...  7.58 us
    ppermute x1, waiting for transfers between devices, on_device(): lax.ppermute(query_in[:, width - rim:].T, 'ctx', [(i, i + 1) for i in ran...  4.26 us
    pallas_call x1, Pallas kernels, on_device(): pl.pallas_call(pack_kernel, out_shape=jax.ShapeDtypeStruct((shards * 17,...  2.57 us
    pallas_call x1, Pallas kernels, on_device(): pl.pallas_call(functools.partial(conv_kernel, rim), out_shape=jax.ShapeDt...  2.1 us
  transfers between devices with their start and end apart: 2, of which 2 were waited for; matrix products, arithmetic and copies ran while one was open for 0% of the time, Pallas kernels for 0%

profile of v4, /device:TPU:33, one launch (start us, length us, event | category | flops | bytes accessed | tf_op | source)
XLA Modules:
  0.0 60.4 jit_solution(16408209428632846371)
XLA Ops:
  0.0 2.6 %pack.1 = f32[1088,128]{1,0:T(8,128)} custom-call(f32[256,256]{1,0:T(8,128)} %key_hbm.1, f32[256,256]{1,0:T(8,128)} %value_hbm.1, f32[256,256]{1,0:T(8,128)} %filter_hbm.1, f32[3,7,256]{2,1,0:T(8,128)} %weight_ref), custom_call_target="tpu_custom_call" | custom-call | tf_op jit(solution)/shard_map/pack/pallas_call | solution.py:290
  2.6 0.0 copy-start
  2.6 0.0 copy-start.7
  2.6 0.0 copy-start.3
  2.6 14.0 %all-to-all-start = ((f32[64,1,2176]{2,1,0:T(1,128)}), f32[64,1,2176]{2,1,0:T(1,128)S(1)}, u32[]{:S(2)}, u32[]{:S(2)}) async-start(f32[64,1,2176]{2,1,0:T(1,128)} %bitcast.9), calls=%async_computation | async-start | bytes 1114112 | tf_op jit(solution)/shard_map/all_to_all | solution.py:312
  16.7 0.0 copy-done
  16.7 0.0 copy-start.1
  16.7 0.1 copy.14
  16.8 7.6 %collective-permute-start = (f32[6,256]{1,0:T(8,128)S(1)}, f32[6,256]{1,0:T(8,128)S(1)}, u32[]{:S(2)}, u32[]{:S(2)}) collective-permute-start(f32[6,256]{1,0:T(8,128)S(1)} %slice_bitcast_fusion), channel_id=1, source_target_pairs={{0,4},{4,8},{8,12},{12,16},{16,20},{20,24},{24,28},{28,32},{32,36}... | collective-permute-start | bytes 18440 | tf_op jit(solution)/shard_map/ppermute | solution.py:315
  24.4 0.0 copy-done.7
  24.4 0.1 dynamic_slice.3.skip_ref
  24.5 0.0 copy-start.2
  24.5 0.0 copy-start.4
  24.5 0.0 copy-start.5
  24.5 0.0 copy-start.6
  24.5 4.3 %collective-permute-done.rim_ref = f32[6,256]{1,0:T(8,128)S(1)} collective-permute-done((f32[6,256]{1,0:T(8,128)S(1)}, f32[6,256]{1,0:T(8,128)S(1)}, u32[]{:S(2)}, u32[]{:S(2)}) %collective-permute-start) | collective-permute-done | bytes 6176 | tf_op jit(solution)/shard_map/ppermute | solution.py:315
  28.8 0.0 copy-done.3
  28.8 0.3 query.1.query_ref
  29.0 10.8 %all-to-all-done = f32[64,1,2176]{2,1,0:T(1,128)S(1)} async-done(((f32[64,1,2176]{2,1,0:T(1,128)}), f32[64,1,2176]{2,1,0:T(1,128)S(1)}, u32[]{:S(2)}, u32[]{:S(2)}) %all-to-all-start) | async-done | bytes 557088 | tf_op jit(solution)/shard_map/all_to_all | solution.py:312
  39.8 0.0 copy-done.1
  39.8 0.0 copy-done.2
  39.8 0.0 copy-done.4
  39.9 0.0 copy-done.5
  39.9 0.0 copy-done.6
  39.9 2.1 %conv.1 = f32[512,128]{1,0:T(8,128)S(1)} custom-call(f32[4]{0:T(128)S(1)} %dynamic_slice.3.skip_ref, f32[1088,128]{1,0:T(8,128)S(1)} %bitcast.6, bf16[128,192]{1,0:T(8,128)(2,1)S(1)} %copy-done.4, bf16[64,384]{1,0:T(8,128)(2,1)S(1)} %copy-done.6, f32[2,64,256]{2,1,0:T(8,128)S(1)} %copy-done.2, f32[2,64,128]{2,1,0:T(8,128)S(1)} %copy-done.5, ...), custom_call_target="tpu_custom_call" | custom-call | tf_op jit(solution)/shard_map/conv/pallas_call | solution.py:330
  42.0 17.7 %all_to_all.10 = f32[64,8,128]{2,1,0:T(8,128)S(1)} all-to-all(f32[64,8,128]{2,1,0:T(8,128)S(1)} %bitcast.8), channel_id=1, replica_groups=mesh['ctx'=64,'grp'=4] {'ctx'}, dimensions={0} | all-to-all | bytes 524288 | tf_op jit(solution)/shard_map/all_to_all | solution.py:344
  59.7 0.7 %gate.1 = f32[256,256]{1,0:T(8,128)} custom-call(f32[256,256]{1,0:T(8,128)S(1)} %query.1.query_ref, f32[512,128]{1,0:T(8,128)S(1)} %bitcast.7), custom_call_target="tpu_custom_call" | custom-call | tf_op jit(solution)/shard_map/gate/pallas_call | solution.py:347
  (1 shorter events, 0.0 us)
Async XLA Ops:
  2.6 14.1 %copy-start = (f32[256,256]{1,0:T(8,128)S(1)}, f32[256,256]{1,0:T(8,128)}, u32[]{:S(2)}) copy-start(f32[256,256]{1,0:T(8,128)} %query_ref) | copy-start | bytes 786436
  2.6 21.8 %copy-start.7 = (f32[256]{0:T(256)S(1)}, f32[256]{0:T(256)}, u32[]{:S(2)}) copy-start(f32[256]{0:T(256)} %param.16) | copy-start | bytes 3076
  2.6 26.2 %copy-start.3 = (f32[3,7,256]{2,1,0:T(8,128)S(1)}, f32[3,7,256]{2,1,0:T(8,128)}, u32[]{:S(2)}) copy-start(f32[3,7,256]{2,1,0:T(8,128)} %weight_ref) | copy-start | bytes 64516
  2.6 37.2 %all-to-all-start = ((f32[64,1,2176]{2,1,0:T(1,128)}), f32[64,1,2176]{2,1,0:T(1,128)S(1)}, u32[]{:S(2)}, u32[]{:S(2)}) async-start(f32[64,1,2176]{2,1,0:T(1,128)} %bitcast.9), calls=%async_computation | async-start | bytes 1114112 | tf_op jit(solution)/shard_map/all_to_all | solution.py:312
  16.7 23.2 %copy-start.1 = (bf16[2,768,256]{2,1,0:T(8,128)(2,1)S(1)}, bf16[2,768,256]{2,1,0:T(8,128)(2,1)}, u32[]{:S(2)}) copy-start(bf16[2,768,256]{2,1,0:T(8,128)(2,1)} %constant.26.clone.dft) | copy-start | bytes 2359300
  16.8 11.9 %collective-permute-start = (f32[6,256]{1,0:T(8,128)S(1)}, f32[6,256]{1,0:T(8,128)S(1)}, u32[]{:S(2)}, u32[]{:S(2)}) collective-permute-start(f32[6,256]{1,0:T(8,128)S(1)} %slice_bitcast_fusion), channel_id=1, source_target_pairs={{0,4},{4,8},{8,12},{12,16},{16,20},{20,24},{24,28},{28,32},{32,36}... | collective-permute-start | bytes 18440 | tf_op jit(solution)/shard_map/ppermute | solution.py:315
  24.5 15.3 %copy-start.2 = (f32[2,64,256]{2,1,0:T(8,128)S(1)}, f32[2,64,256]{2,1,0:T(8,128)}, u32[]{:S(2)}) copy-start(f32[2,64,256]{2,1,0:T(8,128)} %constant.24.clone.turn) | copy-start | bytes 393220
  24.5 15.3 %copy-start.4 = (bf16[128,192]{1,0:T(8,128)(2,1)S(1)}, bf16[128,192]{1,0:T(8,128)(2,1)}, u32[]{:S(2)}) copy-start(bf16[128,192]{1,0:T(8,128)(2,1)} %constant.22.clone.rows_in) | copy-start | bytes 147460
  24.5 15.3 %copy-start.5 = (f32[2,64,128]{2,1,0:T(8,128)S(1)}, f32[2,64,128]{2,1,0:T(8,128)}, u32[]{:S(2)}) copy-start(f32[2,64,128]{2,1,0:T(8,128)} %constant.25.clone.fold) | copy-start | bytes 196612
  24.5 15.4 %copy-start.6 = (bf16[64,384]{1,0:T(8,128)(2,1)S(1)}, bf16[64,384]{1,0:T(8,128)(2,1)}, u32[]{:S(2)}) copy-start(bf16[64,384]{1,0:T(8,128)(2,1)} %constant.23.clone.rows_out) | copy-start | bytes 147460

commit v5 on v4

--- a/solution.py
+++ b/solution.py
@@ -16,7 +16,6 @@
 BF16 = jnp.bfloat16
 VMEM = pl.BlockSpec(memory_space=pltpu.VMEM)
 HBM = pl.BlockSpec(memory_space=pltpu.HBM)
-SMEM = pl.BlockSpec(memory_space=pltpu.SMEM)
 
 
 def halves(table):
@@ -262,9 +261,9 @@
         )
     for c in range(per):
         result = jnp.dot(rows_out[...], values[c], preferred_element_type=F32)
-        result = result + skip_ref[c] * gated[c]
-        out_ref[pl.ds(c, shards, stride=8), :] = result[:, left]
-        out_ref[pl.ds(4 + c, shards, stride=8), :] = result[:, right]
+        skip = skip_ref[c : c + 1, :]
+        out_ref[pl.ds(c, shards, stride=8), :] = result[:, left] + skip * gated[c, :, left]
+        out_ref[pl.ds(4 + c, shards, stride=8), :] = result[:, right] + skip * gated[c, :, right]
 
 
 def gate_kernel(query_ref, conv_ref, out_ref):
@@ -325,12 +324,13 @@
         name="query",
     )(query_in, before, short_weight)
     skip = lax.dynamic_slice(skip_weight, (lax.axis_index("ctx") * per,), (per,))
-    moved, query = lax.optimization_barrier((moved, query))
+    skip = jnp.broadcast_to(skip[:, None], (per, LANES))
+    moved, query, skip = lax.optimization_barrier((moved, query, skip))
     constants = [jnp.asarray(t) for t in tables(shards, width)]
     convolved = pl.pallas_call(
         functools.partial(conv_kernel, rim),
         out_shape=jax.ShapeDtypeStruct((shards * 8, LANES), F32),
-        in_specs=[SMEM] + [VMEM] * 6,
+        in_specs=[VMEM] * 7,
         out_specs=VMEM,
         scratch_shapes=[
             pltpu.VMEM((per, shards, width), F32),

time: 60.7 us -> 60.1 us (level)
  no operation moved by 1% of the time
where the time goes in v5:
time: 60.1 us; the launch traced here: 59.9 us
  starting transfers between devices  21.6 us (36%)
  blocking collectives  17.7 us (29%)
  waiting for transfers between devices  15.1 us (25%)
  Pallas kernels  5.09 us (8%)
    all_to_all x1, blocking collectives, on_device(): lax.all_to_all(convolved.reshape(shards, 8, LANES), 'ctx', split_axis=0,...  17.7 us
    all_to_all x1, starting transfers between devices, on_device(): lax.all_to_all(packed.reshape(shards, 1, 17 * LANES), 'ctx', split_axis=0...  14 us
    all_to_all x1, waiting for transfers between devices, on_device(): lax.all_to_all(packed.reshape(shards, 1, 17 * LANES), 'ctx', split_axis=0...  10.8 us
    ppermute x1, starting transfers between devices, on_device(): lax.ppermute(query_in[:, width - rim:].T, 'ctx', [(i, i + 1) for i in ran...  7.58 us
    ppermute x1, waiting for transfers between devices, on_device(): lax.ppermute(query_in[:, width - rim:].T, 'ctx', [(i, i + 1) for i in ran...  4.26 us
    pallas_call x1, Pallas kernels, on_device(): pl.pallas_call(pack_kernel, out_shape=jax.ShapeDtypeStruct((shards * 17,...  2.57 us
    pallas_call x1, Pallas kernels, on_device(): pl.pallas_call(functools.partial(conv_kernel, rim), out_shape=jax.ShapeDt...  1.51 us
  transfers between devices with their start and end apart: 2, of which 2 were waited for; matrix products, arithmetic and copies ran while one was open for 0% of the time, Pallas kernels for 0%

profile of v5, /device:TPU:33, one launch (start us, length us, event | category | flops | bytes accessed | tf_op | source)
XLA Modules:
  0.0 59.9 jit_solution(2287162469346203433)
XLA Ops:
  0.0 2.6 %pack.1 = f32[1088,128]{1,0:T(8,128)} custom-call(f32[256,256]{1,0:T(8,128)} %key_hbm.1, f32[256,256]{1,0:T(8,128)} %value_hbm.1, f32[256,256]{1,0:T(8,128)} %filter_hbm.1, f32[3,7,256]{2,1,0:T(8,128)} %weight_ref), custom_call_target="tpu_custom_call" | custom-call | tf_op jit(solution)/shard_map/pack/pallas_call | solution.py:289
  2.6 0.0 copy-start
  2.6 0.0 copy-start.7
  2.6 0.0 copy-start.3
  2.6 14.0 %all-to-all-start = ((f32[64,1,2176]{2,1,0:T(1,128)}), f32[64,1,2176]{2,1,0:T(1,128)S(1)}, u32[]{:S(2)}, u32[]{:S(2)}) async-start(f32[64,1,2176]{2,1,0:T(1,128)} %bitcast.9), calls=%async_computation | async-start | bytes 1114112 | tf_op jit(solution)/shard_map/all_to_all | solution.py:311
  16.7 0.0 copy-done
  16.7 0.0 copy-start.1
  16.7 0.1 copy.14
  16.8 7.6 %collective-permute-start = (f32[6,256]{1,0:T(8,128)S(1)}, f32[6,256]{1,0:T(8,128)S(1)}, u32[]{:S(2)}, u32[]{:S(2)}) collective-permute-start(f32[6,256]{1,0:T(8,128)S(1)} %slice_bitcast_fusion), channel_id=1, source_target_pairs={{0,4},{4,8},{8,12},{12,16},{16,20},{20,24},{24,28},{28,32},{32,36}... | collective-permute-start | bytes 18440 | tf_op jit(solution)/shard_map/ppermute | solution.py:314
  24.4 0.0 copy-done.7
  24.4 0.1 dynamic_slice.3
  24.5 0.0 copy-start.2
  24.5 0.0 copy-start.4
  24.5 0.0 copy-start.5
  24.5 0.0 copy-start.6
  24.5 4.3 %collective-permute-done.rim_ref = f32[6,256]{1,0:T(8,128)S(1)} collective-permute-done((f32[6,256]{1,0:T(8,128)S(1)}, f32[6,256]{1,0:T(8,128)S(1)}, u32[]{:S(2)}, u32[]{:S(2)}) %collective-permute-start) | collective-permute-done | bytes 6176 | tf_op jit(solution)/shard_map/ppermute | solution.py:314
  28.8 0.0 copy-done.3
  28.8 0.3 query.1.query_ref
  29.0 10.8 %all-to-all-done = f32[64,1,2176]{2,1,0:T(1,128)S(1)} async-done(((f32[64,1,2176]{2,1,0:T(1,128)}), f32[64,1,2176]{2,1,0:T(1,128)S(1)}, u32[]{:S(2)}, u32[]{:S(2)}) %all-to-all-start) | async-done | bytes 557088 | tf_op jit(solution)/shard_map/all_to_all | solution.py:311
  39.8 0.1 broadcast_in_dim.2.skip_ref
  39.9 0.0 copy-done.1
  39.9 0.0 copy-done.2
  39.9 0.0 copy-done.4
  39.9 0.0 copy-done.5
  39.9 0.0 copy-done.6
  39.9 1.5 %conv.1 = f32[512,128]{1,0:T(8,128)S(1)} custom-call(f32[4,128]{1,0:T(4,128)S(1)} %broadcast_in_dim.2.skip_ref, f32[1088,128]{1,0:T(8,128)S(1)} %bitcast.6, bf16[128,192]{1,0:T(8,128)(2,1)S(1)} %copy-done.4, bf16[64,384]{1,0:T(8,128)(2,1)S(1)} %copy-done.6, f32[2,64,256]{2,1,0:T(8,128)S(1)} %copy-done.2, f32[2,64,128]{2,1,0:T(8,128)S(1)} %copy-done.5, ...), custom_call_target="tpu_custom_call" | custom-call | tf_op jit(solution)/shard_map/conv/pallas_call | solution.py:330
  41.5 17.7 %all_to_all.10 = f32[64,8,128]{2,1,0:T(8,128)S(1)} all-to-all(f32[64,8,128]{2,1,0:T(8,128)S(1)} %bitcast.8), channel_id=1, replica_groups=mesh['ctx'=64,'grp'=4] {'ctx'}, dimensions={0} | all-to-all | bytes 524288 | tf_op jit(solution)/shard_map/all_to_all | solution.py:344
  59.2 0.7 %gate.1 = f32[256,256]{1,0:T(8,128)} custom-call(f32[256,256]{1,0:T(8,128)S(1)} %query.1.query_ref, f32[512,128]{1,0:T(8,128)S(1)} %bitcast.7), custom_call_target="tpu_custom_call" | custom-call | tf_op jit(solution)/shard_map/gate/pallas_call | solution.py:347
  (1 shorter events, 0.0 us)
Async XLA Ops:
  2.6 14.1 %copy-start = (f32[256,256]{1,0:T(8,128)S(1)}, f32[256,256]{1,0:T(8,128)}, u32[]{:S(2)}) copy-start(f32[256,256]{1,0:T(8,128)} %query_ref) | copy-start | bytes 786436
  2.6 21.8 %copy-start.7 = (f32[256]{0:T(256)S(1)}, f32[256]{0:T(256)}, u32[]{:S(2)}) copy-start(f32[256]{0:T(256)} %param.16) | copy-start | bytes 3076
  2.6 26.2 %copy-start.3 = (f32[3,7,256]{2,1,0:T(8,128)S(1)}, f32[3,7,256]{2,1,0:T(8,128)}, u32[]{:S(2)}) copy-start(f32[3,7,256]{2,1,0:T(8,128)} %weight_ref) | copy-start | bytes 64516
  2.6 37.2 %all-to-all-start = ((f32[64,1,2176]{2,1,0:T(1,128)}), f32[64,1,2176]{2,1,0:T(1,128)S(1)}, u32[]{:S(2)}, u32[]{:S(2)}) async-start(f32[64,1,2176]{2,1,0:T(1,128)} %bitcast.9), calls=%async_computation | async-start | bytes 1114112 | tf_op jit(solution)/shard_map/all_to_all | solution.py:311
  16.7 23.3 %copy-start.1 = (bf16[2,768,256]{2,1,0:T(8,128)(2,1)S(1)}, bf16[2,768,256]{2,1,0:T(8,128)(2,1)}, u32[]{:S(2)}) copy-start(bf16[2,768,256]{2,1,0:T(8,128)(2,1)} %constant.26.clone.dft) | copy-start | bytes 2359300
  16.8 11.9 %collective-permute-start = (f32[6,256]{1,0:T(8,128)S(1)}, f32[6,256]{1,0:T(8,128)S(1)}, u32[]{:S(2)}, u32[]{:S(2)}) collective-permute-start(f32[6,256]{1,0:T(8,128)S(1)} %slice_bitcast_fusion), channel_id=1, source_target_pairs={{0,4},{4,8},{8,12},{12,16},{16,20},{20,24},{24,28},{28,32},{32,36}... | collective-permute-start | bytes 18440 | tf_op jit(solution)/shard_map/ppermute | solution.py:314
  24.5 15.4 %copy-start.2 = (f32[2,64,256]{2,1,0:T(8,128)S(1)}, f32[2,64,256]{2,1,0:T(8,128)}, u32[]{:S(2)}) copy-start(f32[2,64,256]{2,1,0:T(8,128)} %constant.24.clone.turn) | copy-start | bytes 393220
  24.5 15.4 %copy-start.4 = (bf16[128,192]{1,0:T(8,128)(2,1)S(1)}, bf16[128,192]{1,0:T(8,128)(2,1)}, u32[]{:S(2)}) copy-start(bf16[128,192]{1,0:T(8,128)(2,1)} %constant.22.clone.rows_in) | copy-start | bytes 147460
  24.5 15.4 %copy-start.5 = (f32[2,64,128]{2,1,0:T(8,128)S(1)}, f32[2,64,128]{2,1,0:T(8,128)}, u32[]{:S(2)}) copy-start(f32[2,64,128]{2,1,0:T(8,128)} %constant.25.clone.fold) | copy-start | bytes 196612
  24.5 15.4 %copy-start.6 = (bf16[64,384]{1,0:T(8,128)(2,1)S(1)}, bf16[64,384]{1,0:T(8,128)(2,1)}, u32[]{:S(2)}) copy-start(bf16[64,384]{1,0:T(8,128)(2,1)} %constant.23.clone.rows_out) | copy-start | bytes 147460

commit v6 on v5

--- a/solution.py
+++ b/solution.py
@@ -1,5 +1,6 @@
 import functools
 import math
+import random
 
 import jax
 import jax.numpy as jnp
@@ -24,18 +25,25 @@
     return high, low
 
 
+def peer_order(count):
+    order = list(range(count))
+    random.Random(1).shuffle(order)
+    return order
+
+
 def split(x):
     high = x.astype(BF16)
     return high, (x - high.astype(F32)).astype(BF16)
 
 
-def tables(blocks, width):
+def tables(blocks, width, order):
     odd = 2 * np.arange(blocks) + 1
     angle = 2.0 * math.pi * (odd[:, None] * np.arange(blocks)[None, :] % (4 * blocks)) / (4 * blocks)
-    high, low = halves(np.concatenate([np.cos(angle), np.sin(angle)], axis=0))
+    arriving = angle[:, order]
+    high, low = halves(np.concatenate([np.cos(arriving), np.sin(arriving)], axis=0))
     rows_in = np.concatenate([high, high, low], axis=1)
     scale = 1.0 / (blocks * width)
-    high, low = halves(np.concatenate([np.cos(angle), np.sin(angle)], axis=0).T * scale)
+    high, low = halves(np.concatenate([np.cos(arriving), np.sin(arriving)], axis=0).T * scale)
     rows_out = np.concatenate([high, high, low], axis=1)
     order = 4 * blocks * width
     turn = 2.0 * math.pi * (odd[:, None] * np.arange(width)[None, :] % order) / order
@@ -176,14 +184,22 @@
 
 
 def conv_kernel(
-    rim, skip_ref, in_ref, rows_in, rows_out, turn, fold, dft, out_ref, gated, first_step, lhs, spec
+    rim, order, skip_ref, in_ref, rows_in, rows_out, turn, fold, dft, out_ref, prior_ref, first_step, lhs, spec
 ):
     shards = in_ref.shape[0] // 17
     per = skip_ref.shape[0]
     lane = lax.broadcasted_iota(jnp.int32, (shards, LANES), 1)
     block = lax.broadcasted_iota(jnp.int32, (shards, LANES), 0)
     line = in_ref[pl.ds(16, shards, stride=17), :]
-    prior = jnp.where(block == 0, 0.0, pltpu.roll(line, 1, 0))
+    for r, here in enumerate(order):
+        if here == 0:
+            start = r
+            prior_ref[r : r + 1, :] = jnp.zeros((1, LANES), F32)
+        else:
+            before = 17 * order.index(here - 1) + 16
+            prior_ref[r : r + 1, :] = in_ref[before : before + 1, :]
+    prior = prior_ref[...]
+    zero_lag = (block == start) & (lane == 0)
     left, right = slice(0, LANES), slice(LANES, 2 * LANES)
 
     def triple(value):
@@ -203,15 +219,12 @@
         first = in_ref[pl.ds(c, shards, stride=17), :]
         first = jnp.where(lane < rim, (first + key_spill) * (here + value_spill), first)
         second = in_ref[pl.ds(4 + c, shards, stride=17), :]
-        gated[c, :, left] = first
-        gated[c, :, right] = second
         signals.append(jnp.concatenate([first, second], axis=1))
     for c in range(per):
-        signals.append(
-            jnp.concatenate(
-                [in_ref[pl.ds(8 + h * 4 + c, shards, stride=17), :] for h in range(2)], axis=1
-            )
-        )
+        first = in_ref[pl.ds(8 + c, shards, stride=17), :]
+        first = first + jnp.where(zero_lag, skip_ref[c : c + 1, :], 0.0)
+        second = in_ref[pl.ds(12 + c, shards, stride=17), :]
+        signals.append(jnp.concatenate([first, second], axis=1))
     for n, signal in enumerate(signals):
         first_step[n] = jnp.dot(rows_in[...], triple(signal), preferred_element_type=F32)
     count = 2 * per * shards
@@ -261,9 +274,8 @@
         )
     for c in range(per):
         result = jnp.dot(rows_out[...], values[c], preferred_element_type=F32)
-        skip = skip_ref[c : c + 1, :]
-        out_ref[pl.ds(c, shards, stride=8), :] = result[:, left] + skip * gated[c, :, left]
-        out_ref[pl.ds(4 + c, shards, stride=8), :] = result[:, right] + skip * gated[c, :, right]
+        out_ref[pl.ds(c, shards, stride=8), :] = result[:, left]
+        out_ref[pl.ds(4 + c, shards, stride=8), :] = result[:, right]
 
 
 def gate_kernel(query_ref, conv_ref, out_ref):
@@ -285,6 +297,7 @@
     rim = short_weight.shape[1] - 1
     shards = lax.axis_size("ctx")
     per = channels // shards
+    order = peer_order(shards)
     rows = pltpu.VMEM((2, width + 16, LANES), F32)
     packed = pl.pallas_call(
         pack_kernel,
@@ -309,7 +322,12 @@
     )(key_in, value_in, long_filter, short_weight)
     packed, query_in, short_weight = lax.optimization_barrier((packed, query_in, short_weight))
     moved = lax.all_to_all(
-        packed.reshape(shards, 1, 17 * LANES), "ctx", split_axis=0, concat_axis=0, tiled=True
+        packed.reshape(shards, 1, 17 * LANES),
+        "ctx",
+        split_axis=0,
+        concat_axis=0,
+        axis_index_groups=[order],
+        tiled=True,
     ).reshape(shards * 17, LANES)
     before = lax.ppermute(
         query_in[:, width - rim :].T, "ctx", [(i, i + 1) for i in range(shards - 1)]
@@ -323,17 +341,18 @@
         compiler_params=limit(8),
         name="query",
     )(query_in, before, short_weight)
-    skip = lax.dynamic_slice(skip_weight, (lax.axis_index("ctx") * per,), (per,))
+    rank = jnp.asarray(np.argsort(order), jnp.int32)[lax.axis_index("ctx")]
+    skip = lax.dynamic_slice(skip_weight, (rank * per,), (per,))
     skip = jnp.broadcast_to(skip[:, None], (per, LANES))
     moved, query, skip = lax.optimization_barrier((moved, query, skip))
-    constants = [jnp.asarray(t) for t in tables(shards, width)]
+    constants = [jnp.asarray(t) for t in tables(shards, width, order)]
     convolved = pl.pallas_call(
-        functools.partial(conv_kernel, rim),
+        functools.partial(conv_kernel, rim, order),
         out_shape=jax.ShapeDtypeStruct((shards * 8, LANES), F32),
         in_specs=[VMEM] * 7,
         out_specs=VMEM,
         scratch_shapes=[
-            pltpu.VMEM((per, shards, width), F32),
+            pltpu.VMEM((shards, LANES), F32),
             pltpu.VMEM((2 * per, 2 * shards, width), F32),
             pltpu.VMEM((4 * channels, 3 * width), BF16),
             pltpu.VMEM((4 * channels, width), F32),
@@ -342,7 +361,12 @@
         name="conv",
     )(skip, moved, *constants)
     returned = lax.all_to_all(
-        convolved.reshape(shards, 8, LANES), "ctx", split_axis=0, concat_axis=0, tiled=True
+        convolved.reshape(shards, 8, LANES),
+        "ctx",
+        split_axis=0,
+        concat_axis=0,
+        axis_index_groups=[order],
+        tiled=True,
     ).reshape(shards * 8, LANES)
     return pl.pallas_call(
         gate_kernel,

time: 60.1 us -> 56.9 us (0.947)
  starting transfers between devices: 21.6 us -> 17 us
  blocking collectives: 17.7 us -> 20.3 us
  waiting for transfers between devices: 15.1 us -> 12.5 us
  between operations: 0.12 us -> 0.79 us
    all_to_all x1, waiting for transfers between devices: 10.8 us -> 4.45 us  [on_device(): lax.all_to_all(packed.reshape(shards, 1, 17 * LANES), 'ctx', split_axis=0...]
    ppermute x1, starting transfers between devices: 7.58 us -> 2.43 us  [on_device(): lax.ppermute(query_in[:, width - rim:].T, 'ctx', [(i, i + 1) for i in ran...]
    ppermute x1, waiting for transfers between devices: 4.26 us -> 8.08 us  [on_device(): lax.ppermute(query_in[:, width - rim:].T, 'ctx', [(i, i + 1) for i in ran...]
    all_to_all x1, blocking collectives: 17.7 us -> 20.3 us  [on_device(): lax.all_to_all(convolved.reshape(shards, 8, LANES), 'ctx', split_axis=0,...]
  transfers between devices with their start and end apart: 2 -> 2, of which waited for: 2 -> 2; matrix products, arithmetic and copies ran while one was open for 0% -> 1% of each run, Pallas kernels for 0% -> 0%
where the time goes in v6:
time: 56.9 us; the launch traced here: 56.7 us
  blocking collectives  20.3 us (36%)
  starting transfers between devices  17 us (30%)
  waiting for transfers between devices  12.5 us (22%)
  Pallas kernels  5.11 us (9%)
  local copies, waits for them, and re-layouts  0.91 us (2%)
  between operations  0.79 us (1%)
    all_to_all x1, blocking collectives, on_device(): lax.all_to_all(convolved.reshape(shards, 8, LANES), 'ctx', split_axis=0,...  20.3 us
    all_to_all x1, starting transfers between devices, on_device(): lax.all_to_all(packed.reshape(shards, 1, 17 * LANES), 'ctx', split_axis=0...  14.6 us
    ppermute x1, waiting for transfers between devices, on_device(): lax.ppermute(query_in[:, width - rim:].T, 'ctx', [(i, i + 1) for i in ran...  8.08 us
    all_to_all x1, waiting for transfers between devices, on_device(): lax.all_to_all(packed.reshape(shards, 1, 17 * LANES), 'ctx', split_axis=0...  4.45 us
    pallas_call x1, Pallas kernels, on_device(): pl.pallas_call(pack_kernel, out_shape=jax.ShapeDtypeStruct((shards * 17,...  2.58 us
    ppermute x1, starting transfers between devices, on_device(): lax.ppermute(query_in[:, width - rim:].T, 'ctx', [(i, i + 1) for i in ran...  2.43 us
    pallas_call x1, Pallas kernels, on_device(): pl.pallas_call(functools.partial(conv_kernel, rim, order), out_shape=jax....  1.53 us
  transfers between devices with their start and end apart: 2, of which 2 were waited for; matrix products, arithmetic and copies ran while one was open for 1% of the time, Pallas kernels for 0%

profile of v6, /device:TPU:33, one launch (start us, length us, event | category | flops | bytes accessed | tf_op | source)
XLA Modules:
  0.0 56.7 jit_solution(18217554983433910083)
XLA Ops:
  0.0 2.6 %pack.1 = f32[1088,128]{1,0:T(8,128)} custom-call(f32[256,256]{1,0:T(8,128)} %key_hbm.1, f32[256,256]{1,0:T(8,128)} %value_hbm.1, f32[256,256]{1,0:T(8,128)} %filter_hbm.1, f32[3,7,256]{2,1,0:T(8,128)} %weight_ref), custom_call_target="tpu_custom_call" | custom-call | tf_op jit(solution)/shard_map/pack/pallas_call | solution.py:302
  2.6 0.0 copy-start
  2.6 0.0 copy-start.8
  2.6 0.0 copy-start.7
  2.6 0.0 copy-start.3
  2.6 14.6 %all-to-all-start = ((f32[64,1,2176]{2,1,0:T(1,128)}), f32[64,1,2176]{2,1,0:T(1,128)S(1)}, u32[]{:S(2)}, u32[]{:S(2)}) async-start(f32[64,1,2176]{2,1,0:T(1,128)} %bitcast.10), calls=%async_computation | async-start | bytes 1114112 | tf_op jit(solution)/shard_map/all_to_all | solution.py:324
  17.2 0.0 copy-done
  17.2 0.0 copy-start.1
  17.2 0.1 copy.15
  17.4 2.4 %collective-permute-start = (f32[6,256]{1,0:T(8,128)S(1)}, f32[6,256]{1,0:T(8,128)S(1)}, u32[]{:S(2)}, u32[]{:S(2)}) collective-permute-start(f32[6,256]{1,0:T(8,128)S(1)} %slice_bitcast_fusion), channel_id=1, source_target_pairs={{0,4},{4,8},{8,12},{12,16},{16,20},{20,24},{24,28},{28,32},{32,36}... | collective-permute-start | bytes 18440 | tf_op jit(solution)/shard_map/ppermute | solution.py:332
  19.8 0.0 copy-done.8
  19.8 0.6 %dynamic_slice.6 = s32[1]{0:T(128)} dynamic-slice(s32[64]{0:T(128)S(1)} %copy-done.8, s32[]{:T(128)S(6)} %select_n.6), dynamic_slice_sizes={1} | dynamic-slice | bytes 12 | tf_op jit(solution)/shard_map/dynamic_slice | solution.py:344
  21.1 0.0 copy-done.7
  21.1 0.1 dynamic_slice.7
  21.1 0.0 copy-start.2
  21.1 0.0 copy-start.4
  21.1 0.0 copy-start.5
  21.1 0.0 copy-start.6
  21.2 8.1 %collective-permute-done.rim_ref = f32[6,256]{1,0:T(8,128)S(1)} collective-permute-done((f32[6,256]{1,0:T(8,128)S(1)}, f32[6,256]{1,0:T(8,128)S(1)}, u32[]{:S(2)}, u32[]{:S(2)}) %collective-permute-start) | collective-permute-done | bytes 6176 | tf_op jit(solution)/shard_map/ppermute | solution.py:332
  29.2 0.0 copy-done.3
  29.2 0.3 query.1.query_ref
  29.5 4.4 %all-to-all-done = f32[64,1,2176]{2,1,0:T(1,128)S(1)} async-done(((f32[64,1,2176]{2,1,0:T(1,128)}), f32[64,1,2176]{2,1,0:T(1,128)S(1)}, u32[]{:S(2)}, u32[]{:S(2)}) %all-to-all-start) | async-done | bytes 557088 | tf_op jit(solution)/shard_map/all_to_all | solution.py:324
  34.0 0.1 broadcast_in_dim.2.skip_ref
  34.0 0.0 copy-done.1
  34.0 0.0 copy-done.2
  34.0 0.0 copy-done.4
  34.0 0.0 copy-done.5
  34.0 0.0 copy-done.6
  34.1 1.5 %conv.1 = f32[512,128]{1,0:T(8,128)S(1)} custom-call(f32[4,128]{1,0:T(4,128)S(1)} %broadcast_in_dim.2.skip_ref, f32[1088,128]{1,0:T(8,128)S(1)} %bitcast.7, bf16[128,192]{1,0:T(8,128)(2,1)S(1)} %copy-done.4, bf16[64,384]{1,0:T(8,128)(2,1)S(1)} %copy-done.6, f32[2,64,256]{2,1,0:T(8,128)S(1)} %copy-done.2, f32[2,64,128]{2,1,0:T(8,128)S(1)} %copy-done.5, ...), custom_call_target="tpu_custom_call" | custom-call | tf_op jit(solution)/shard_map/conv/pallas_call | solution.py:349
  35.6 20.3 %all_to_all.10 = f32[64,8,128]{2,1,0:T(8,128)S(1)} all-to-all(f32[64,8,128]{2,1,0:T(8,128)S(1)} %bitcast.9), channel_id=1, replica_groups={{88,48,208,12,76,20,240,232,8,132,40,32,116,104,100,36,176,72,248,44,18..., dimensions={0} | all-to-all | bytes 524288 | tf_op jit(solution)/shard_map/all_to_all | solution.py:363
  55.9 0.7 %gate.1 = f32[256,256]{1,0:T(8,128)} custom-call(f32[256,256]{1,0:T(8,128)S(1)} %query.1.query_ref, f32[512,128]{1,0:T(8,128)S(1)} %bitcast.8), custom_call_target="tpu_custom_call" | custom-call | tf_op jit(solution)/shard_map/gate/pallas_call | solution.py:371
  (1 shorter events, 0.0 us)
Async XLA Ops:
  2.6 14.6 %copy-start = (f32[256,256]{1,0:T(8,128)S(1)}, f32[256,256]{1,0:T(8,128)}, u32[]{:S(2)}) copy-start(f32[256,256]{1,0:T(8,128)} %query_ref) | copy-start | bytes 786436
  2.6 17.2 %copy-start.8 = (s32[64]{0:T(128)S(1)}, s32[64]{0:T(128)}, u32[]{:S(2)}) copy-start(s32[64]{0:T(128)} %constant.27.clone) | copy-start | bytes 772
  2.6 18.4 %copy-start.7 = (f32[256]{0:T(256)S(1)}, f32[256]{0:T(256)}, u32[]{:S(2)}) copy-start(f32[256]{0:T(256)} %param.17) | copy-start | bytes 3076
  2.6 26.6 %copy-start.3 = (f32[3,7,256]{2,1,0:T(8,128)S(1)}, f32[3,7,256]{2,1,0:T(8,128)}, u32[]{:S(2)}) copy-start(f32[3,7,256]{2,1,0:T(8,128)} %weight_ref) | copy-start | bytes 64516
  2.6 31.3 %all-to-all-start = ((f32[64,1,2176]{2,1,0:T(1,128)}), f32[64,1,2176]{2,1,0:T(1,128)S(1)}, u32[]{:S(2)}, u32[]{:S(2)}) async-start(f32[64,1,2176]{2,1,0:T(1,128)} %bitcast.10), calls=%async_computation | async-start | bytes 1114112 | tf_op jit(solution)/shard_map/all_to_all | solution.py:324
  17.2 16.8 %copy-start.1 = (bf16[2,768,256]{2,1,0:T(8,128)(2,1)S(1)}, bf16[2,768,256]{2,1,0:T(8,128)(2,1)}, u32[]{:S(2)}) copy-start(bf16[2,768,256]{2,1,0:T(8,128)(2,1)} %constant.32.clone.dft) | copy-start | bytes 2359300
  17.4 11.9 %collective-permute-start = (f32[6,256]{1,0:T(8,128)S(1)}, f32[6,256]{1,0:T(8,128)S(1)}, u32[]{:S(2)}, u32[]{:S(2)}) collective-permute-start(f32[6,256]{1,0:T(8,128)S(1)} %slice_bitcast_fusion), channel_id=1, source_target_pairs={{0,4},{4,8},{8,12},{12,16},{16,20},{20,24},{24,28},{28,32},{32,36}... | collective-permute-start | bytes 18440 | tf_op jit(solution)/shard_map/ppermute | solution.py:332
  21.1 12.9 %copy-start.2 = (f32[2,64,256]{2,1,0:T(8,128)S(1)}, f32[2,64,256]{2,1,0:T(8,128)}, u32[]{:S(2)}) copy-start(f32[2,64,256]{2,1,0:T(8,128)} %constant.30.clone.turn) | copy-start | bytes 393220
  21.1 12.9 %copy-start.4 = (bf16[128,192]{1,0:T(8,128)(2,1)S(1)}, bf16[128,192]{1,0:T(8,128)(2,1)}, u32[]{:S(2)}) copy-start(bf16[128,192]{1,0:T(8,128)(2,1)} %constant.28.clone.rows_in) | copy-start | bytes 147460
  21.1 12.9 %copy-start.5 = (f32[2,64,128]{2,1,0:T(8,128)S(1)}, f32[2,64,128]{2,1,0:T(8,128)}, u32[]{:S(2)}) copy-start(f32[2,64,128]{2,1,0:T(8,128)} %constant.31.clone.fold) | copy-start | bytes 196612
  21.1 12.9 %copy-start.6 = (bf16[64,384]{1,0:T(8,128)(2,1)S(1)}, bf16[64,384]{1,0:T(8,128)(2,1)}, u32[]{:S(2)}) copy-start(bf16[64,384]{1,0:T(8,128)(2,1)} %constant.29.clone.rows_out) | copy-start | bytes 147460

commit v7 on v6

--- a/solution.py
+++ b/solution.py
@@ -27,7 +27,7 @@
 
 def peer_order(count):
     order = list(range(count))
-    random.Random(1).shuffle(order)
+    random.Random(21).shuffle(order)
     return order
 
 

time: 56.9 us -> 55.4 us (0.974)
  waiting for transfers between devices: 12.5 us -> 10.9 us
    all_to_all x1, waiting for transfers between devices: 4.45 us -> 3.4 us  [on_device(): lax.all_to_all(packed.reshape(shards, 1, 17 * LANES), 'ctx', split_axis=0...]
where the time goes in v7:
time: 55.4 us; the launch traced here: 55.1 us
  blocking collectives  20.2 us (36%)
  starting transfers between devices  17.2 us (31%)
  waiting for transfers between devices  10.9 us (20%)
  Pallas kernels  5.11 us (9%)
  local copies, waits for them, and re-layouts  0.91 us (2%)
  between operations  0.79 us (1%)
    all_to_all x1, blocking collectives, on_device(): lax.all_to_all(convolved.reshape(shards, 8, LANES), 'ctx', split_axis=0,...  20.2 us
    all_to_all x1, starting transfers between devices, on_device(): lax.all_to_all(packed.reshape(shards, 1, 17 * LANES), 'ctx', split_axis=0...  14.4 us
    ppermute x1, waiting for transfers between devices, on_device(): lax.ppermute(query_in[:, width - rim:].T, 'ctx', [(i, i + 1) for i in ran...  7.55 us
    all_to_all x1, waiting for transfers between devices, on_device(): lax.all_to_all(packed.reshape(shards, 1, 17 * LANES), 'ctx', split_axis=0...  3.4 us
    ppermute x1, starting transfers between devices, on_device(): lax.ppermute(query_in[:, width - rim:].T, 'ctx', [(i, i + 1) for i in ran...  2.73 us
    pallas_call x1, Pallas kernels, on_device(): pl.pallas_call(pack_kernel, out_shape=jax.ShapeDtypeStruct((shards * 17,...  2.58 us
    pallas_call x1, Pallas kernels, on_device(): pl.pallas_call(functools.partial(conv_kernel, rim, order), out_shape=jax....  1.53 us
  transfers between devices with their start and end apart: 2, of which 2 were waited for; matrix products, arithmetic and copies ran while one was open for 1% of the time, Pallas kernels for 0%

profile of v7, /device:TPU:33, one launch (start us, length us, event | category | flops | bytes accessed | tf_op | source)
XLA Modules:
  0.0 55.1 jit_solution(14974202844297244385)
XLA Ops:
  0.0 2.6 %pack.1 = f32[1088,128]{1,0:T(8,128)} custom-call(f32[256,256]{1,0:T(8,128)} %key_hbm.1, f32[256,256]{1,0:T(8,128)} %value_hbm.1, f32[256,256]{1,0:T(8,128)} %filter_hbm.1, f32[3,7,256]{2,1,0:T(8,128)} %weight_ref), custom_call_target="tpu_custom_call" | custom-call | tf_op jit(solution)/shard_map/pack/pallas_call | solution.py:302
  2.6 0.0 copy-start
  2.6 0.0 copy-start.8
  2.6 0.0 copy-start.7
  2.6 0.0 copy-start.3
  2.6 14.4 %all-to-all-start = ((f32[64,1,2176]{2,1,0:T(1,128)}), f32[64,1,2176]{2,1,0:T(1,128)S(1)}, u32[]{:S(2)}, u32[]{:S(2)}) async-start(f32[64,1,2176]{2,1,0:T(1,128)} %bitcast.10), calls=%async_computation | async-start | bytes 1114112 | tf_op jit(solution)/shard_map/all_to_all | solution.py:324
  17.1 0.0 copy-done
  17.1 0.0 copy-start.1
  17.1 0.1 copy.15
  17.3 2.7 %collective-permute-start = (f32[6,256]{1,0:T(8,128)S(1)}, f32[6,256]{1,0:T(8,128)S(1)}, u32[]{:S(2)}, u32[]{:S(2)}) collective-permute-start(f32[6,256]{1,0:T(8,128)S(1)} %slice_bitcast_fusion), channel_id=1, source_target_pairs={{0,4},{4,8},{8,12},{12,16},{16,20},{20,24},{24,28},{28,32},{32,36}... | collective-permute-start | bytes 18440 | tf_op jit(solution)/shard_map/ppermute | solution.py:332
  20.0 0.0 copy-done.8
  20.0 0.6 %dynamic_slice.6 = s32[1]{0:T(128)} dynamic-slice(s32[64]{0:T(128)S(1)} %copy-done.8, s32[]{:T(128)S(6)} %select_n.6), dynamic_slice_sizes={1} | dynamic-slice | bytes 12 | tf_op jit(solution)/shard_map/dynamic_slice | solution.py:344
  21.3 0.0 copy-done.7
  21.3 0.1 dynamic_slice.7
  21.3 0.0 copy-start.2
  21.3 0.0 copy-start.4
  21.3 0.0 copy-start.5
  21.3 0.0 copy-start.6
  21.3 7.6 %collective-permute-done.rim_ref = f32[6,256]{1,0:T(8,128)S(1)} collective-permute-done((f32[6,256]{1,0:T(8,128)S(1)}, f32[6,256]{1,0:T(8,128)S(1)}, u32[]{:S(2)}, u32[]{:S(2)}) %collective-permute-start) | collective-permute-done | bytes 6176 | tf_op jit(solution)/shard_map/ppermute | solution.py:332
  28.9 0.0 copy-done.3
  28.9 0.3 query.1.query_ref
  29.2 3.4 %all-to-all-done = f32[64,1,2176]{2,1,0:T(1,128)S(1)} async-done(((f32[64,1,2176]{2,1,0:T(1,128)}), f32[64,1,2176]{2,1,0:T(1,128)S(1)}, u32[]{:S(2)}, u32[]{:S(2)}) %all-to-all-start) | async-done | bytes 557088 | tf_op jit(solution)/shard_map/all_to_all | solution.py:324
  32.6 0.1 broadcast_in_dim.2.skip_ref
  32.6 0.0 copy-done.1
  32.6 0.0 copy-done.2
  32.7 0.0 copy-done.4
  32.7 0.0 copy-done.5
  32.7 0.0 copy-done.6
  32.7 1.5 %conv.1 = f32[512,128]{1,0:T(8,128)S(1)} custom-call(f32[4,128]{1,0:T(4,128)S(1)} %broadcast_in_dim.2.skip_ref, f32[1088,128]{1,0:T(8,128)S(1)} %bitcast.7, bf16[128,192]{1,0:T(8,128)(2,1)S(1)} %copy-done.4, bf16[64,384]{1,0:T(8,128)(2,1)S(1)} %copy-done.6, f32[2,64,256]{2,1,0:T(8,128)S(1)} %copy-done.2, f32[2,64,128]{2,1,0:T(8,128)S(1)} %copy-done.5, ...), custom_call_target="tpu_custom_call" | custom-call | tf_op jit(solution)/shard_map/conv/pallas_call | solution.py:349
  34.2 20.2 %all_to_all.10 = f32[64,8,128]{2,1,0:T(8,128)S(1)} all-to-all(f32[64,8,128]{2,1,0:T(8,128)S(1)} %bitcast.9), channel_id=1, replica_groups={{220,24,64,144,100,76,32,236,4,224,28,196,232,136,96,188,48,40,68,20,15..., dimensions={0} | all-to-all | bytes 524288 | tf_op jit(solution)/shard_map/all_to_all | solution.py:363
  54.4 0.7 %gate.1 = f32[256,256]{1,0:T(8,128)} custom-call(f32[256,256]{1,0:T(8,128)S(1)} %query.1.query_ref, f32[512,128]{1,0:T(8,128)S(1)} %bitcast.8), custom_call_target="tpu_custom_call" | custom-call | tf_op jit(solution)/shard_map/gate/pallas_call | solution.py:371
  (1 shorter events, 0.0 us)
Async XLA Ops:
  2.6 14.5 %copy-start = (f32[256,256]{1,0:T(8,128)S(1)}, f32[256,256]{1,0:T(8,128)}, u32[]{:S(2)}) copy-start(f32[256,256]{1,0:T(8,128)} %query_ref) | copy-start | bytes 786436
  2.6 17.4 %copy-start.8 = (s32[64]{0:T(128)S(1)}, s32[64]{0:T(128)}, u32[]{:S(2)}) copy-start(s32[64]{0:T(128)} %constant.27.clone) | copy-start | bytes 772
  2.6 18.6 %copy-start.7 = (f32[256]{0:T(256)S(1)}, f32[256]{0:T(256)}, u32[]{:S(2)}) copy-start(f32[256]{0:T(256)} %param.17) | copy-start | bytes 3076
  2.6 26.3 %copy-start.3 = (f32[3,7,256]{2,1,0:T(8,128)S(1)}, f32[3,7,256]{2,1,0:T(8,128)}, u32[]{:S(2)}) copy-start(f32[3,7,256]{2,1,0:T(8,128)} %weight_ref) | copy-start | bytes 64516
  2.6 29.9 %all-to-all-start = ((f32[64,1,2176]{2,1,0:T(1,128)}), f32[64,1,2176]{2,1,0:T(1,128)S(1)}, u32[]{:S(2)}, u32[]{:S(2)}) async-start(f32[64,1,2176]{2,1,0:T(1,128)} %bitcast.10), calls=%async_computation | async-start | bytes 1114112 | tf_op jit(solution)/shard_map/all_to_all | solution.py:324
  17.1 15.6 %copy-start.1 = (bf16[2,768,256]{2,1,0:T(8,128)(2,1)S(1)}, bf16[2,768,256]{2,1,0:T(8,128)(2,1)}, u32[]{:S(2)}) copy-start(bf16[2,768,256]{2,1,0:T(8,128)(2,1)} %constant.32.clone.dft) | copy-start | bytes 2359300
  17.3 11.6 %collective-permute-start = (f32[6,256]{1,0:T(8,128)S(1)}, f32[6,256]{1,0:T(8,128)S(1)}, u32[]{:S(2)}, u32[]{:S(2)}) collective-permute-start(f32[6,256]{1,0:T(8,128)S(1)} %slice_bitcast_fusion), channel_id=1, source_target_pairs={{0,4},{4,8},{8,12},{12,16},{16,20},{20,24},{24,28},{28,32},{32,36}... | collective-permute-start | bytes 18440 | tf_op jit(solution)/shard_map/ppermute | solution.py:332
  21.3 11.3 %copy-start.2 = (f32[2,64,256]{2,1,0:T(8,128)S(1)}, f32[2,64,256]{2,1,0:T(8,128)}, u32[]{:S(2)}) copy-start(f32[2,64,256]{2,1,0:T(8,128)} %constant.30.clone.turn) | copy-start | bytes 393220
  21.3 11.3 %copy-start.4 = (bf16[128,192]{1,0:T(8,128)(2,1)S(1)}, bf16[128,192]{1,0:T(8,128)(2,1)}, u32[]{:S(2)}) copy-start(bf16[128,192]{1,0:T(8,128)(2,1)} %constant.28.clone.rows_in) | copy-start | bytes 147460
  21.3 11.3 %copy-start.5 = (f32[2,64,128]{2,1,0:T(8,128)S(1)}, f32[2,64,128]{2,1,0:T(8,128)}, u32[]{:S(2)}) copy-start(f32[2,64,128]{2,1,0:T(8,128)} %constant.31.clone.fold) | copy-start | bytes 196612
  21.3 11.3 %copy-start.6 = (bf16[64,384]{1,0:T(8,128)(2,1)S(1)}, bf16[64,384]{1,0:T(8,128)(2,1)}, u32[]{:S(2)}) copy-start(bf16[64,384]{1,0:T(8,128)(2,1)} %constant.29.clone.rows_out) | copy-start | bytes 147460

commit v8 on v7

--- a/solution.py
+++ b/solution.py
@@ -27,7 +27,7 @@
 
 def peer_order(count):
     order = list(range(count))
-    random.Random(21).shuffle(order)
+    random.Random(16).shuffle(order)
     return order
 
 

time: 55.4 us -> 56.2 us (1.014)
  waiting for transfers between devices: 10.9 us -> 12.6 us
    all_to_all x1, waiting for transfers between devices: 3.4 us -> 4.73 us  [on_device(): lax.all_to_all(packed.reshape(shards, 1, 17 * LANES), 'ctx', split_axis=0...]
where the time goes in v8:
time: 56.2 us; the launch traced here: 55.9 us
  blocking collectives  19.8 us (35%)
  starting transfers between devices  16.7 us (30%)
  waiting for transfers between devices  12.6 us (22%)
  Pallas kernels  5.11 us (9%)
  local copies, waits for them, and re-layouts  0.91 us (2%)
  between operations  0.79 us (1%)
    all_to_all x1, blocking collectives, on_device(): lax.all_to_all(convolved.reshape(shards, 8, LANES), 'ctx', split_axis=0,...  19.8 us
    all_to_all x1, starting transfers between devices, on_device(): lax.all_to_all(packed.reshape(shards, 1, 17 * LANES), 'ctx', split_axis=0...  14.2 us
    ppermute x1, waiting for transfers between devices, on_device(): lax.ppermute(query_in[:, width - rim:].T, 'ctx', [(i, i + 1) for i in ran...  7.87 us
    all_to_all x1, waiting for transfers between devices, on_device(): lax.all_to_all(packed.reshape(shards, 1, 17 * LANES), 'ctx', split_axis=0...  4.73 us
    pallas_call x1, Pallas kernels, on_device(): pl.pallas_call(pack_kernel, out_shape=jax.ShapeDtypeStruct((shards * 17,...  2.58 us
    ppermute x1, starting transfers between devices, on_device(): lax.ppermute(query_in[:, width - rim:].T, 'ctx', [(i, i + 1) for i in ran...  2.5 us
    pallas_call x1, Pallas kernels, on_device(): pl.pallas_call(functools.partial(conv_kernel, rim, order), out_shape=jax....  1.53 us
  transfers between devices with their start and end apart: 2, of which 2 were waited for; matrix products, arithmetic and copies ran while one was open for 1% of the time, Pallas kernels for 0%

profile of v8, /device:TPU:33, one launch (start us, length us, event | category | flops | bytes accessed | tf_op | source)
XLA Modules:
  0.0 55.9 jit_solution(3639500591976445560)
XLA Ops:
  0.0 2.6 %pack.1 = f32[1088,128]{1,0:T(8,128)} custom-call(f32[256,256]{1,0:T(8,128)} %key_hbm.1, f32[256,256]{1,0:T(8,128)} %value_hbm.1, f32[256,256]{1,0:T(8,128)} %filter_hbm.1, f32[3,7,256]{2,1,0:T(8,128)} %weight_ref), custom_call_target="tpu_custom_call" | custom-call | tf_op jit(solution)/shard_map/pack/pallas_call | solution.py:302
  2.6 0.0 copy-start
  2.6 0.0 copy-start.8
  2.6 0.0 copy-start.7
  2.6 0.0 copy-start.3
  2.6 14.2 %all-to-all-start = ((f32[64,1,2176]{2,1,0:T(1,128)}), f32[64,1,2176]{2,1,0:T(1,128)S(1)}, u32[]{:S(2)}, u32[]{:S(2)}) async-start(f32[64,1,2176]{2,1,0:T(1,128)} %bitcast.10), calls=%async_computation | async-start | bytes 1114112 | tf_op jit(solution)/shard_map/all_to_all | solution.py:324
  16.9 0.0 copy-done
  16.9 0.0 copy-start.1
  16.9 0.1 copy.15
  17.0 2.5 %collective-permute-start = (f32[6,256]{1,0:T(8,128)S(1)}, f32[6,256]{1,0:T(8,128)S(1)}, u32[]{:S(2)}, u32[]{:S(2)}) collective-permute-start(f32[6,256]{1,0:T(8,128)S(1)} %slice_bitcast_fusion), channel_id=1, source_target_pairs={{0,4},{4,8},{8,12},{12,16},{16,20},{20,24},{24,28},{28,32},{32,36}... | collective-permute-start | bytes 18440 | tf_op jit(solution)/shard_map/ppermute | solution.py:332
  19.5 0.0 copy-done.8
  19.5 0.6 %dynamic_slice.6 = s32[1]{0:T(128)} dynamic-slice(s32[64]{0:T(128)S(1)} %copy-done.8, s32[]{:T(128)S(6)} %select_n.6), dynamic_slice_sizes={1} | dynamic-slice | bytes 12 | tf_op jit(solution)/shard_map/dynamic_slice | solution.py:344
  20.8 0.0 copy-done.7
  20.8 0.1 dynamic_slice.7
  20.9 0.0 copy-start.2
  20.9 0.0 copy-start.4
  20.9 0.0 copy-start.5
  20.9 0.0 copy-start.6
  20.9 7.9 %collective-permute-done.rim_ref = f32[6,256]{1,0:T(8,128)S(1)} collective-permute-done((f32[6,256]{1,0:T(8,128)S(1)}, f32[6,256]{1,0:T(8,128)S(1)}, u32[]{:S(2)}, u32[]{:S(2)}) %collective-permute-start) | collective-permute-done | bytes 6176 | tf_op jit(solution)/shard_map/ppermute | solution.py:332
  28.8 0.0 copy-done.3
  28.8 0.3 query.1.query_ref
  29.0 4.7 %all-to-all-done = f32[64,1,2176]{2,1,0:T(1,128)S(1)} async-done(((f32[64,1,2176]{2,1,0:T(1,128)}), f32[64,1,2176]{2,1,0:T(1,128)S(1)}, u32[]{:S(2)}, u32[]{:S(2)}) %all-to-all-start) | async-done | bytes 557088 | tf_op jit(solution)/shard_map/all_to_all | solution.py:324
  33.8 0.1 broadcast_in_dim.2.skip_ref
  33.8 0.0 copy-done.1
  33.8 0.0 copy-done.2
  33.8 0.0 copy-done.4
  33.8 0.0 copy-done.5
  33.8 0.0 copy-done.6
  33.9 1.5 %conv.1 = f32[512,128]{1,0:T(8,128)S(1)} custom-call(f32[4,128]{1,0:T(4,128)S(1)} %broadcast_in_dim.2.skip_ref, f32[1088,128]{1,0:T(8,128)S(1)} %bitcast.7, bf16[128,192]{1,0:T(8,128)(2,1)S(1)} %copy-done.4, bf16[64,384]{1,0:T(8,128)(2,1)S(1)} %copy-done.6, f32[2,64,256]{2,1,0:T(8,128)S(1)} %copy-done.2, f32[2,64,128]{2,1,0:T(8,128)S(1)} %copy-done.5, ...), custom_call_target="tpu_custom_call" | custom-call | tf_op jit(solution)/shard_map/conv/pallas_call | solution.py:349
  35.4 19.8 %all_to_all.10 = f32[64,8,128]{2,1,0:T(8,128)S(1)} all-to-all(f32[64,8,128]{2,1,0:T(8,128)S(1)} %bitcast.9), channel_id=1, replica_groups={{92,40,24,16,88,96,164,244,12,196,220,188,48,176,80,68,136,228,124,20,1..., dimensions={0} | all-to-all | bytes 524288 | tf_op jit(solution)/shard_map/all_to_all | solution.py:363
  55.2 0.7 %gate.1 = f32[256,256]{1,0:T(8,128)} custom-call(f32[256,256]{1,0:T(8,128)S(1)} %query.1.query_ref, f32[512,128]{1,0:T(8,128)S(1)} %bitcast.8), custom_call_target="tpu_custom_call" | custom-call | tf_op jit(solution)/shard_map/gate/pallas_call | solution.py:371
  (1 shorter events, 0.0 us)
Async XLA Ops:
  2.6 14.3 %copy-start = (f32[256,256]{1,0:T(8,128)S(1)}, f32[256,256]{1,0:T(8,128)}, u32[]{:S(2)}) copy-start(f32[256,256]{1,0:T(8,128)} %query_ref) | copy-start | bytes 786436
  2.6 16.9 %copy-start.8 = (s32[64]{0:T(128)S(1)}, s32[64]{0:T(128)}, u32[]{:S(2)}) copy-start(s32[64]{0:T(128)} %constant.27.clone) | copy-start | bytes 772
  2.6 18.2 %copy-start.7 = (f32[256]{0:T(256)S(1)}, f32[256]{0:T(256)}, u32[]{:S(2)}) copy-start(f32[256]{0:T(256)} %param.17) | copy-start | bytes 3076
  2.6 26.1 %copy-start.3 = (f32[3,7,256]{2,1,0:T(8,128)S(1)}, f32[3,7,256]{2,1,0:T(8,128)}, u32[]{:S(2)}) copy-start(f32[3,7,256]{2,1,0:T(8,128)} %weight_ref) | copy-start | bytes 64516
  2.6 31.1 %all-to-all-start = ((f32[64,1,2176]{2,1,0:T(1,128)}), f32[64,1,2176]{2,1,0:T(1,128)S(1)}, u32[]{:S(2)}, u32[]{:S(2)}) async-start(f32[64,1,2176]{2,1,0:T(1,128)} %bitcast.10), calls=%async_computation | async-start | bytes 1114112 | tf_op jit(solution)/shard_map/all_to_all | solution.py:324
  16.9 17.0 %copy-start.1 = (bf16[2,768,256]{2,1,0:T(8,128)(2,1)S(1)}, bf16[2,768,256]{2,1,0:T(8,128)(2,1)}, u32[]{:S(2)}) copy-start(bf16[2,768,256]{2,1,0:T(8,128)(2,1)} %constant.32.clone.dft) | copy-start | bytes 2359300
  17.0 11.7 %collective-permute-start = (f32[6,256]{1,0:T(8,128)S(1)}, f32[6,256]{1,0:T(8,128)S(1)}, u32[]{:S(2)}, u32[]{:S(2)}) collective-permute-start(f32[6,256]{1,0:T(8,128)S(1)} %slice_bitcast_fusion), channel_id=1, source_target_pairs={{0,4},{4,8},{8,12},{12,16},{16,20},{20,24},{24,28},{28,32},{32,36}... | collective-permute-start | bytes 18440 | tf_op jit(solution)/shard_map/ppermute | solution.py:332
  20.9 13.0 %copy-start.2 = (f32[2,64,256]{2,1,0:T(8,128)S(1)}, f32[2,64,256]{2,1,0:T(8,128)}, u32[]{:S(2)}) copy-start(f32[2,64,256]{2,1,0:T(8,128)} %constant.30.clone.turn) | copy-start | bytes 393220
  20.9 13.0 %copy-start.4 = (bf16[128,192]{1,0:T(8,128)(2,1)S(1)}, bf16[128,192]{1,0:T(8,128)(2,1)}, u32[]{:S(2)}) copy-start(bf16[128,192]{1,0:T(8,128)(2,1)} %constant.28.clone.rows_in) | copy-start | bytes 147460
  20.9 13.0 %copy-start.5 = (f32[2,64,128]{2,1,0:T(8,128)S(1)}, f32[2,64,128]{2,1,0:T(8,128)}, u32[]{:S(2)}) copy-start(f32[2,64,128]{2,1,0:T(8,128)} %constant.31.clone.fold) | copy-start | bytes 196612
  20.9 13.0 %copy-start.6 = (bf16[64,384]{1,0:T(8,128)(2,1)S(1)}, bf16[64,384]{1,0:T(8,128)(2,1)}, u32[]{:S(2)}) copy-start(bf16[64,384]{1,0:T(8,128)(2,1)} %constant.29.clone.rows_out) | copy-start | bytes 147460
